TPU v7x, 32 devices: a whole 2x2x4 slice. The times are simulated.
32 devices in a mesh: dp: 8 (over z, y), mp: 4 (over x, core).
Axes of the slice: x: 2, y: 2, z: 4, core: 2. Of those that a mesh axis runs over, the one named last changes fastest.
Arguments:
- frames: bfloat16 [8192, 320], P('dp'), may hold values from -6 to 6
- lengths: int32 [8, 128], P('dp'), may hold values from 0 to 15, as said below
- destinations: int32 [8, 128], P('dp'), may hold values from 0 to 7, as said below
- offsets: int32 [8, 128], P('dp'), may hold values from 0 to 255, as said below
- in_weight: bfloat16 [320, 1536], P(None, 'mp'), may hold values from -0.3125 to 0.3125
- depth_weight: bfloat16 [31, 1536], P(None, 'mp'), may hold values from -1 to 1
- out_weight: bfloat16 [1536, 1536], P(None, 'mp'), may hold values from -0.15625 to 0.15625
- cotangent: bfloat16 [2048, 1536], P('dp', 'mp'), may hold values from -6 to 6
Outputs:
- output: bfloat16 [2048, 1536], P('dp', 'mp')
- in_weight_gradient: float32 [320, 1536], P(None, 'mp')
- depth_gradient: float32 [31, 1536], P(None, 'mp')
- out_weight_gradient: float32 [1536, 1536], P('dp', 'mp')
Inputs may be any that keep to these rules, and one draw needn't show every extreme that they name: Used entries of a device's list come first and have lengths of 1 or more; later entries have length 0; some utterance has exactly 15 rows. `destinations`: A device's utterances for one destination stand together and fill exactly 128 rows; unused entries name device 0; some device sends to every device. `offsets`: the utterances sent to one device tile its 256 rows exactly; unused entries have offset 0; on every device some utterance starts at row 255.
All inputs are finite; a program needn't handle non-finite values.
Results may differ from a plain program's by a relative error of at most 0.014.
Values may be sent and summed in bfloat16 or wider, within the bound.
A program may use at most 64 MiB of HBM per device.

v0:
```python
import math

import jax
import jax.numpy as jnp
from jax import lax
from jax.sharding import PartitionSpec as P

KERNEL = 31
ROWS = 256


def depth_conv(values, weights, labels, direction):
    center = (KERNEL - 1) // 2
    length = values.shape[0]
    padded = jnp.pad(values, ((center, center), (0, 0)))
    padded_labels = jnp.pad(labels, (center, center), constant_values=-1)
    result = jnp.zeros(values.shape, jnp.float32)
    for tap_index in range(KERNEL):
        start = center + direction * (tap_index - center)
        matches = (padded_labels[start : start + length] == labels)[:, None]
        taken = weights[tap_index][None, :] * padded[start : start + length]
        result = result + jnp.where(matches, taken, jnp.zeros_like(taken))
    return result


def tap_sums(grads, values, labels):
    center = (KERNEL - 1) // 2
    length = values.shape[0]
    padded = jnp.pad(values, ((center, center), (0, 0)))
    padded_labels = jnp.pad(labels, (center, center), constant_values=-1)
    rows_list = []
    for tap_index in range(KERNEL):
        matches = (padded_labels[tap_index : tap_index + length] == labels)[:, None]
        taken = grads * padded[tap_index : tap_index + length]
        rows_list.append(jnp.sum(jnp.where(matches, taken, jnp.zeros_like(taken)), axis=0))
    return jnp.stack(rows_list, 0)


def per_device(
    frames, lengths, destinations, offsets, in_weight, depth_weight, out_weight, cotangent
):
    dp_count = lax.axis_size("dp")
    src_rows = frames.shape[0]
    features = frames.shape[1]
    slot_rows = src_rows // dp_count
    entries = lengths.shape[1]
    lengths_row = lengths[0]
    end_rows = jnp.cumsum(lengths_row, dtype=jnp.int32)
    begins = end_rows - lengths_row
    row_ids = jnp.arange(src_rows, dtype=jnp.int32)
    owner_table = (begins[None, :] <= row_ids[:, None]) & (row_ids[:, None] < end_rows[None, :])
    occupied_rows = jnp.any(owner_table, axis=1)
    onehot = owner_table.astype(jnp.int32)

    def lookup(table):
        return jnp.sum(onehot * table[None, :], axis=1, dtype=jnp.int32)

    owner_index = lookup(jnp.arange(entries, dtype=jnp.int32))
    target = lookup(offsets[0]) + row_ids - lookup(begins)
    dest_row = lookup(destinations[0])
    source = lax.axis_index("dp")
    row_label = source * entries + owner_index
    dump_index = dp_count * slot_rows
    slot_index = jnp.where(occupied_rows, dest_row * slot_rows + row_ids % slot_rows, dump_index)
    send_frames = (
        jnp.zeros((dump_index + 1, features), frames.dtype)
        .at[slot_index]
        .set(frames)[:dump_index]
        .reshape(dp_count, slot_rows, features)
    )
    send_target = (
        jnp.full((dump_index + 1,), ROWS, jnp.int32)
        .at[slot_index]
        .set(target)[:dump_index]
        .reshape(dp_count, slot_rows)
    )
    send_label = (
        jnp.full((dump_index + 1,), -1, jnp.int32)
        .at[slot_index]
        .set(row_label)[:dump_index]
        .reshape(dp_count, slot_rows)
    )
    got_frames, got_target, got_label = (
        lax.all_to_all(send_frames, "dp", split_axis=0, concat_axis=0, tiled=True),
        lax.all_to_all(send_target, "dp", split_axis=0, concat_axis=0, tiled=True),
        lax.all_to_all(send_label, "dp", split_axis=0, concat_axis=0, tiled=True),
    )
    flat_target = got_target.reshape(-1)
    packed = (
        jnp.zeros((ROWS + 1, features), frames.dtype)
        .at[flat_target]
        .set(got_frames.reshape(-1, features))[:ROWS]
    )
    packed_labels = (
        jnp.full((ROWS + 1,), -1, jnp.int32).at[flat_target].set(got_label.reshape(-1))[:ROWS]
    )
    hidden = jnp.dot(packed, in_weight, preferred_element_type=jnp.float32).astype(jnp.bfloat16)
    hidden_wide = hidden.astype(jnp.float32)
    taps = depth_weight.astype(jnp.float32)
    convolved = depth_conv(hidden_wide, taps, packed_labels, 1)
    activated = jax.nn.silu(convolved).astype(jnp.bfloat16)
    partial_sum = lax.dot_general(
        activated, out_weight, (((1,), (1,)), ((), ())), preferred_element_type=jnp.float32
    )
    branch = lax.psum_scatter(
        partial_sum.astype(jnp.bfloat16), "mp", scatter_dimension=1, tiled=True
    ).astype(jnp.float32)
    output = (hidden_wide + branch).astype(jnp.bfloat16)
    cotangent_full = lax.all_gather(cotangent, "mp", axis=1, tiled=True)
    grad_scale = 1.0 / math.sqrt(dp_count * ROWS)
    grad_activated = jnp.dot(cotangent_full, out_weight, preferred_element_type=jnp.float32)
    sigmoid_value = jax.nn.sigmoid(convolved)
    grad_convolved = grad_activated * sigmoid_value * (1.0 + convolved * (1.0 - sigmoid_value))
    grad_hidden = (
        cotangent.astype(jnp.float32) + depth_conv(grad_convolved, taps, packed_labels, -1)
    ).astype(jnp.bfloat16)
    out_weight_gradient = lax.psum_scatter(
        grad_scale
        * lax.dot_general(
            cotangent_full, activated, (((0,), (0,)), ((), ())), preferred_element_type=jnp.float32
        ),
        "dp",
        scatter_dimension=0,
        tiled=True,
    )
    term_in = grad_scale * lax.dot_general(
        packed, grad_hidden, (((0,), (0,)), ((), ())), preferred_element_type=jnp.float32
    )
    term_depth = grad_scale * tap_sums(grad_convolved, hidden_wide, packed_labels)
    in_weight_gradient, depth_gradient = lax.psum((term_in, term_depth), "dp")
    return (output, in_weight_gradient, depth_gradient, out_weight_gradient)


def solution(mesh):
    placed = (
        P("dp", None),
        P("dp", None),
        P("dp", None),
        P("dp", None),
        P(None, "mp"),
        P(None, "mp"),
        P(None, "mp"),
        P("dp", "mp"),
    )
    return jax.shard_map(
        per_device,
        mesh=mesh,
        in_specs=placed,
        out_specs=(P("dp", "mp"), P(None, "mp"), P(None, "mp"), P("dp", "mp")),
        check_vma=False,
    )
```

profile of v0, /device:TPU:0, one launch (start us, length us, event | category | flops | bytes accessed | tf_op | source)
XLA Modules:
  0.0 261.1 jit_solution(8230476609553892758)
XLA Ops:
  10.6 4.3 %scatter_custom_fusion = s32[1025]{0:T(1024)S(1)} fusion(s32[1024]{0:T(1024)S(1)} %bitcast.42, s32[1024]{0:T(1024)S(1)} %get-tuple-element.126, s32[]{:T(128)} %constant.21.clone.1), kind=kCustom, calls=%fused_computation.253 | custom fusion | bytes 4104 | tf_op jit(solution)/shard_map/scatter | solution.py:74
  15.5 7.3 %all-to-all-start = ((s32[8,1,128]{2,1,0:T(1,128)}), s32[8,1,128]{2,1,0:T(1,128)S(1)}, u32[]{:S(2)}, u32[]{:S(2)}) async-start(s32[8,1,128]{2,1,0:T(1,128)} %bitcast.6), calls=%async_computation | async-start | bytes 8192 | tf_op jit(solution)/shard_map/all_to_all | solution.py:85
  22.8 4.3 %scatter_custom_fusion.3 = s32[1025]{0:T(1024)S(1)} fusion(s32[1024]{0:T(1024)S(1)} %bitcast.43, s32[1024]{0:T(1024)S(1)} %get-tuple-element.127, s32[]{:T(128)} %constant.56.clone.1), kind=kCustom, calls=%fused_computation.250 | custom fusion | bytes 4104 | tf_op jit(solution)/shard_map/scatter | solution.py:80
  27.7 1.5 all-to-all-done
  29.2 4.5 %all-to-all-start.2 = ((s32[8,1,128]{2,1,0:T(1,128)}), s32[8,1,128]{2,1,0:T(1,128)S(1)}, u32[]{:S(2)}, u32[]{:S(2)}) async-start(s32[8,1,128]{2,1,0:T(1,128)} %bitcast.11), calls=%async_computation.2 | async-start | bytes 8192 | tf_op jit(solution)/shard_map/all_to_all | solution.py:86
  33.7 1.4 copy.33
  35.1 5.2 %scatter_custom_fusion.1 = bf16[1025,320]{1,0:T(8,128)(2,1)S(1)} fusion(s32[1024]{0:T(1024)S(1)} %bitcast.44, bf16[1024,320]{1,0:T(8,128)(2,1)S(1)} %copy.33, bf16[]{:T(256)} %constant.20.clone.1), kind=kCustom, calls=%fused_computation.20 | custom fusion | bytes 656002 | tf_op jit(solution)/shard_map/scatter | solution.py:68
  41.6 6.0 %all-to-all-start.1 = ((bf16[8,128,320]{1,2,0:T(8,128)(2,1)}), bf16[8,128,320]{1,2,0:T(8,128)(2,1)S(1)}, u32[]{:S(2)}, u32[]{:S(2)}) async-start(bf16[8,128,320]{1,2,0:T(8,128)(2,1)} %copy.34), calls=%async_computation.1 | async-start | bytes 1310720 | tf_op jit(solution)/shard_map/all_to_all | solution.py:84
  48.1 4.3 %scatter_custom_fusion.4 = s32[257]{0:T(512)S(1)} fusion(s32[1024]{0:T(1024)S(1)} %bitcast.40, s32[1024]{0:T(1024)S(1)} %bitcast.39, s32[]{:T(128)} %constant.56.clone.1), kind=kCustom, calls=%fused_computation.318 | custom fusion | bytes 1032 | tf_op jit(solution)/shard_map/scatter | solution.py:95
  53.9 9.9 %all-to-all-done.1 = bf16[8,128,320]{1,2,0:T(8,128)(2,1)S(1)} async-done(((bf16[8,128,320]{1,2,0:T(8,128)(2,1)}), bf16[8,128,320]{1,2,0:T(8,128)(2,1)S(1)}, u32[]{:S(2)}, u32[]{:S(2)}) %all-to-all-start.1) | async-done | bytes 655392 | tf_op jit(solution)/shard_map/all_to_all | solution.py:84
  64.1 5.1 %scatter_custom_fusion.2 = bf16[257,320]{1,0:T(8,128)(2,1)S(1)} fusion(s32[1024]{0:T(1024)S(1)} %bitcast.41, bf16[1024,320]{1,0:T(8,128)(2,1)S(1)} %bitcast.36, bf16[]{:T(256)} %constant.20.clone.1), kind=kCustom, calls=%fused_computation.211 | custom fusion | bytes 164482 | tf_op jit(solution)/shard_map/scatter | solution.py:92
  69.9 4.0 %select_add_fusion = f32[256,384]{1,0:T(8,128)S(1)} fusion(f32[256,384]{1,0:T(8,128)S(1)} %fusion.2, f32[384]{0:T(512)S(1)} %get-tuple-element.60, f32[384]{0:T(512)S(1)} %get-tuple-element.61, f32[384]{0:T(512)S(1)} %get-tuple-element.62, f32[384]{0:T(512)S(1)} %get-tuple-element.63, f32[384]{0:T(512)S(1)} %get-tuple-element.64, ...), kind=kLoop, calls=%fused_computation.207 | loop fusion | flops 8945664 | bytes 841728 | tf_op jit(solution)/shard_map/add | solution.py:22
  75.8 8.6 %all_gather.3 = bf16[256,1536]{1,0:T(8,128)(2,1)S(1)} all-gather(bf16[256,384]{1,0:T(8,128)(2,1)S(1)} %copy-done.2), channel_id=1, replica_groups=mesh['dp'=8,'mp'=4] {'mp'}, dimensions={1}, use_global_device_ids=true | all-gather | bytes 983040 | tf_op jit(solution)/shard_map/all_gather | solution.py:109
  84.4 13.8 %reduce-scatter.7.cloned.1.call-done = bf16[384,256]{1,0:T(8,128)(2,1)} async-done(((bf16[1536,256]{1,0:T(8,128)(2,1)}), bf16[384,256]{1,0:T(8,128)(2,1)}) %reduce-scatter.7.cloned.1.call-update) | async-done | bytes 196624
  99.7 3.5 %select_reduce_fusion.13 = (f32[384]{0:T(512)}, f32[384]{0:T(512)}, f32[384]{0:T(512)}, f32[384]{0:T(512)}, f32[384]{0:T(512)}, /*index=5*/f32[384]{0:T(512)}, f...) fusion(f32[256,384]{1,0:T(8,128)S(1)} %fusion.2, ...), kind=kOutput, calls=%fused_computation.182 | convolution fusion | flops 305623680 | bytes 3554816 | tf_op jit(solution)/shard_map/dot_general | solution.py:111
  103.6 4.2 %convolution_multiply_fusion.1 = f32[320,384]{1,0:T(8,128)} fusion(f32[256,384]{1,0:T(8,128)S(1)} %get-tuple-element.125, bf16[256,384]{1,0:T(8,128)(2,1)S(1)} %copy-done.3, f32[384]{0:T(512)S(1)} %get-tuple-element.60, f32[384]{0:T(512)S(1)} %copy-done.6, f32[384]{0:T(512)S(1)} %copy-done.8, f32[384]{0:T(512)S(1)} %copy-done.10, f32[384]{0:T(512)S(1)} %copy-done.12, ...), kind=kOutput, calls=%fused_computation.8 | convolution fusion | flops 72278016 | bytes 1351680 | tf_op jit(solution)/shard_map/dot_general | solution.py:126
  107.8 1.9 fusion
  109.8 3.1 %copy.41 = f32[1536,384]{1,0:T(8,128)} copy(f32[1536,384]{0,1:T(8,128)} %fusion) | data formatting | bytes 4718592
  114.1 1.6 select_reduce_fusion.4
  115.8 1.6 select_reduce_fusion.21
  117.7 38.2 %psum.15 = f32[31,384]{1,0:T(8,128)} all-reduce(f32[31,384]{1,0:T(8,128)S(1)} %broadcast_multiply_fusion), channel_id=1, replica_groups=mesh['dp'=8,'mp'=4] {'dp'}, use_global_device_ids=true, to_apply=%region_44.45 | all-reduce | flops 11904 | bytes 95232 | tf_op jit(solution)/shard_map/psum | solution.py:130
  155.9 24.4 %all-reduce.5.cloned.1.call-done = f32[320,384]{1,0:T(8,128)} async-done(((f32[320,384]{1,0:T(8,128)}), f32[320,384]{1,0:T(8,128)}) %all-reduce.5.cloned.1.call-update) | async-done | bytes 491536 | tf_op jit(solution)/shard_map/psum | solution.py:130
  180.3 72.4 %reduce-scatter.9.cloned.1.call-done = f32[192,384]{1,0:T(8,128)} async-done(((f32[1536,384]{1,0:T(8,128)}), f32[192,384]{1,0:T(8,128)}) %reduce-scatter.9.cloned.1.call-update) | async-done | bytes 294928
  252.7 1.8 copy.45
  (270 shorter events, 12.4 us)
Async XLA Ops:
  7.2 66.8 %copy-start = (bf16[1536,384]{1,0:T(8,128)(2,1)S(1)}, bf16[1536,384]{1,0:T(8,128)(2,1)}, u32[]{:S(2)}) copy-start(bf16[1536,384]{1,0:T(8,128)(2,1)} %param.14) | copy-start | bytes 3538948
  15.5 13.7 %all-to-all-start = ((s32[8,1,128]{2,1,0:T(1,128)}), s32[8,1,128]{2,1,0:T(1,128)S(1)}, u32[]{:S(2)}, u32[]{:S(2)}) async-start(s32[8,1,128]{2,1,0:T(1,128)} %bitcast.6), calls=%async_computation | async-start | bytes 8192 | tf_op jit(solution)/shard_map/all_to_all | solution.py:85
  29.2 12.4 %all-to-all-start.2 = ((s32[8,1,128]{2,1,0:T(1,128)}), s32[8,1,128]{2,1,0:T(1,128)S(1)}, u32[]{:S(2)}, u32[]{:S(2)}) async-start(s32[8,1,128]{2,1,0:T(1,128)} %bitcast.11), calls=%async_computation.2 | async-start | bytes 8192 | tf_op jit(solution)/shard_map/all_to_all | solution.py:86
  41.6 22.2 %all-to-all-start.1 = ((bf16[8,128,320]{1,2,0:T(8,128)(2,1)}), bf16[8,128,320]{1,2,0:T(8,128)(2,1)S(1)}, u32[]{:S(2)}, u32[]{:S(2)}) async-start(bf16[8,128,320]{1,2,0:T(8,128)(2,1)} %copy.34), calls=%async_computation.1 | async-start | bytes 1310720 | tf_op jit(solution)/shard_map/all_to_all | solution.py:84
  47.6 50.7 %reduce-scatter.7.cloned.1.call-start = ((), (), s32[]{:S(2)}) async-start(), calls=%async_computation.6 | async-start | bytes 983040
  47.7 21.9 %copy-start.39 = (f32[384]{0:T(512)}, f32[384]{0:T(512)S(1)}, u32[]{:S(2)}) copy-start(f32[384]{0:T(512)S(1)} %get-tuple-element.78) | copy-start | bytes 4612
  47.7 21.9 %copy-start.41 = (f32[384]{0:T(512)}, f32[384]{0:T(512)S(1)}, u32[]{:S(2)}) copy-start(f32[384]{0:T(512)S(1)} %get-tuple-element.79) | copy-start | bytes 4612
  47.7 21.9 %copy-start.43 = (f32[384]{0:T(512)}, f32[384]{0:T(512)S(1)}, u32[]{:S(2)}) copy-start(f32[384]{0:T(512)S(1)} %get-tuple-element.80) | copy-start | bytes 4612
  47.7 21.9 %copy-start.45 = (f32[384]{0:T(512)}, f32[384]{0:T(512)S(1)}, u32[]{:S(2)}) copy-start(f32[384]{0:T(512)S(1)} %get-tuple-element.81) | copy-start | bytes 4612
  47.7 21.9 %copy-start.47 = (f32[384]{0:T(512)}, f32[384]{0:T(512)S(1)}, u32[]{:S(2)}) copy-start(f32[384]{0:T(512)S(1)} %get-tuple-element.82) | copy-start | bytes 4612
  47.7 21.9 %copy-start.49 = (f32[384]{0:T(512)}, f32[384]{0:T(512)S(1)}, u32[]{:S(2)}) copy-start(f32[384]{0:T(512)S(1)} %get-tuple-element.83) | copy-start | bytes 4612
  47.8 21.9 %copy-start.51 = (f32[384]{0:T(512)}, f32[384]{0:T(512)S(1)}, u32[]{:S(2)}) copy-start(f32[384]{0:T(512)S(1)} %get-tuple-element.84) | copy-start | bytes 4612
  47.8 21.9 %copy-start.53 = (f32[384]{0:T(512)}, f32[384]{0:T(512)S(1)}, u32[]{:S(2)}) copy-start(f32[384]{0:T(512)S(1)} %get-tuple-element.85) | copy-start | bytes 4612
  47.8 21.9 %copy-start.55 = (f32[384]{0:T(512)}, f32[384]{0:T(512)S(1)}, u32[]{:S(2)}) copy-start(f32[384]{0:T(512)S(1)} %get-tuple-element.86) | copy-start | bytes 4612
  47.8 21.9 %copy-start.57 = (f32[384]{0:T(512)}, f32[384]{0:T(512)S(1)}, u32[]{:S(2)}) copy-start(f32[384]{0:T(512)S(1)} %get-tuple-element.87) | copy-start | bytes 4612
  47.8 21.9 %copy-start.59 = (f32[384]{0:T(512)}, f32[384]{0:T(512)S(1)}, u32[]{:S(2)}) copy-start(f32[384]{0:T(512)S(1)} %get-tuple-element.88) | copy-start | bytes 4612
  47.8 21.9 %copy-start.61 = (f32[384]{0:T(512)}, f32[384]{0:T(512)S(1)}, u32[]{:S(2)}) copy-start(f32[384]{0:T(512)S(1)} %get-tuple-element.89) | copy-start | bytes 4612
  47.9 21.8 %copy-start.5 = (f32[384]{0:T(512)}, f32[384]{0:T(512)S(1)}, u32[]{:S(2)}) copy-start(f32[384]{0:T(512)S(1)} %get-tuple-element.61) | copy-start | bytes 4612
  47.9 21.8 %copy-start.7 = (f32[384]{0:T(512)}, f32[384]{0:T(512)S(1)}, u32[]{:S(2)}) copy-start(f32[384]{0:T(512)S(1)} %get-tuple-element.62) | copy-start | bytes 4612
  47.9 21.8 %copy-start.9 = (f32[384]{0:T(512)}, f32[384]{0:T(512)S(1)}, u32[]{:S(2)}) copy-start(f32[384]{0:T(512)S(1)} %get-tuple-element.63) | copy-start | bytes 4612
  48.0 21.8 %copy-start.11 = (f32[384]{0:T(512)}, f32[384]{0:T(512)S(1)}, u32[]{:S(2)}) copy-start(f32[384]{0:T(512)S(1)} %get-tuple-element.64) | copy-start | bytes 4612
  48.0 21.8 %copy-start.13 = (f32[384]{0:T(512)}, f32[384]{0:T(512)S(1)}, u32[]{:S(2)}) copy-start(f32[384]{0:T(512)S(1)} %get-tuple-element.65) | copy-start | bytes 4612
  75.7 104.6 %all-reduce.5.cloned.1.call-start = ((), (), s32[]{:S(2)}) async-start(), calls=%async_computation.5 | async-start | bytes 983040 | tf_op jit(solution)/shard_map/psum | solution.py:130
  107.8 144.9 %reduce-scatter.9.cloned.1.call-start = ((), (), s32[]{:S(2)}) async-start(), calls=%async_computation.7 | async-start | bytes 2654208
  (84 other events, 640.1 us)
Sparse Core Ops, SparseCore 0:
  75.9 22.3 reduce-scatter.6
  107.9 72.3 all-reduce.4
  184.4 68.3 reduce-scatter.8
where the time goes:
time: 262 us; the launch traced here: 261 us
  waiting for transfers between devices  122 us (47%)
  blocking collectives  46.8 us (18%)
  local copies, waits for them, and re-layouts  36.8 us (14%)
  starting transfers between devices  17.9 us (7%)
  between operations  15.7 us (6%)
  other arithmetic  11.4 us (4%)
  matrix products  10.5 us (4%)
    unnamed x5, waiting for transfers between devices  86.3 us
    psum x1, blocking collectives, per_device(): in_weight_gradient, depth_gradient = lax.psum((term_in, term_depth), 'dp')  38.2 us
    psum x1, waiting for transfers between devices, per_device(): in_weight_gradient, depth_gradient = lax.psum((term_in, term_depth), 'dp')  24.4 us
    all_to_all x1, waiting for transfers between devices, per_device(): lax.all_to_all(send_frames, 'dp', split_axis=0, concat_axis=0, tiled=True)  9.89 us
    unnamed x209, local copies, waits for them, and re-layouts  9.52 us
    all_gather x1, blocking collectives, per_device(): cotangent_full = lax.all_gather(cotangent, 'mp', axis=1, tiled=True)  8.6 us
    all_to_all x1, starting transfers between devices, per_device(): lax.all_to_all(send_target, 'dp', split_axis=0, concat_axis=0, tiled=True)  7.28 us
    all_to_all x1, starting transfers between devices, per_device(): lax.all_to_all(send_frames, 'dp', split_axis=0, concat_axis=0, tiled=True)  6 us
  transfers between devices with their start and end apart: 6, of which 5 were waited for; matrix products, arithmetic and copies ran while one was open for 10% of the time, Pallas kernels for 0%

commit v1 on v0

--- a/solution.py
+++ b/solution.py
@@ -1,12 +1,16 @@
+import functools
 import math
 
 import jax
 import jax.numpy as jnp
 from jax import lax
+from jax.experimental import pallas as pl
+from jax.experimental.pallas import tpu as pltpu
 from jax.sharding import PartitionSpec as P
 
 KERNEL = 31
 ROWS = 256
+MESH = pl.DeviceIdType.MESH
 
 
 def depth_conv(values, weights, labels, direction):
@@ -131,7 +135,355 @@
     return (output, in_weight_gradient, depth_gradient, out_weight_gradient)
 
 
+def fused_kernel(
+    n_dp, n_mp, scale,
+    frames, lens, dests, offs, w_in, w_depth, w_out, cot,
+    out_ref, gin_ref, gdep_ref, gout_ref,
+    tables, slots, got, comp_all, cot_all, cot_t, packed, lab_pad, masks, taps, hpad, act, gact, gpad, ghid,
+    part, part_got, dy_send, dy_got, dz_send, dz_got, dz_own, gfull, gs, ggot, gall,
+    tab_s, tab_r, fr_s, fr_r, cp_s, cp_r, ct_s, ct_r, pt_s, pt_r, dy_s, dy_r, dz_s, dz_r, gr_s, gr_r, ga_s, ga_r,
+):
+    f32, bf16 = jnp.float32, jnp.bfloat16
+    me = lax.axis_index("dp")
+    mine = lax.axis_index("mp")
+    src_rows, features = frames.shape
+    slot_rows = src_rows // n_dp
+    quarter = slot_rows // n_mp
+    sources = ROWS // slot_rows
+    width = cot.shape[1]
+    entries = lens.shape[1]
+    block = gout_ref.shape[0]
+    strip = gs.shape[1]
+    centre = (KERNEL - 1) // 2
+    pad = 16
+    n_z = n_dp // 2
+    zi, yi = me // 2, lax.rem(me, 2)
+    chunk = 64
+
+    def dp_peer(k):
+        return lax.rem(me + k, n_dp)
+
+    def dp_from(k):
+        return lax.rem(me + n_dp - k, n_dp)
+
+    def mp_peer(k):
+        return lax.rem(mine + k, n_mp)
+
+    def mp_from(k):
+        return lax.rem(mine + n_mp - k, n_mp)
+
+    def send(src, dst, ssem, rsem, **where):
+        return pltpu.make_async_remote_copy(
+            src_ref=src, dst_ref=dst, send_sem=ssem, recv_sem=rsem, device_id=where, device_id_type=MESH
+        )
+
+    barrier = pltpu.get_barrier_semaphore()
+    for k in range(1, n_dp):
+        pl.semaphore_signal(barrier, inc=1, device_id={"dp": dp_peer(k)}, device_id_type=MESH)
+    for k in range(1, n_mp):
+        pl.semaphore_signal(barrier, inc=1, device_id={"mp": mp_peer(k)}, device_id_type=MESH)
+
+    len_f = lens[...].astype(f32)
+    dest_f = dests[...].astype(f32)
+    off_f = offs[...].astype(f32)
+    before = (
+        lax.broadcasted_iota(jnp.int32, (entries, entries), 0) < lax.broadcasted_iota(jnp.int32, (entries, entries), 1)
+    )
+    begin_f = jnp.dot(
+        jnp.broadcast_to(len_f, (8, entries)).astype(bf16), jnp.where(before, 1.0, 0.0).astype(bf16),
+        preferred_element_type=f32,
+    )[0:1]
+    tables[me] = jnp.concatenate([len_f, dest_f, off_f, begin_f, jnp.zeros((4, entries), f32)], 0)
+    row = lax.broadcasted_iota(jnp.int32, (n_dp * quarter, 1), 0)
+    row_dest = (row // quarter).astype(f32)
+    row_in = lax.rem(row, quarter).astype(f32)
+    first = jnp.min(jnp.where((dest_f == row_dest) & (len_f > 0.0), begin_f, 1e6), axis=1, keepdims=True)
+    wanted = first + row_in + (mine * quarter).astype(f32)
+    cols = lax.broadcasted_iota(jnp.int32, (n_dp * quarter, src_rows), 1).astype(f32)
+    pick = jnp.where(cols == wanted, 1.0, 0.0).astype(bf16)
+    chosen = jnp.dot(pick, frames[...], preferred_element_type=f32).astype(bf16)
+    for d in range(n_dp):
+        slots[d] = chosen[d * quarter : (d + 1) * quarter]
+    got[me] = slots[me]
+    cot_all[mine] = cot[...]
+
+    pl.semaphore_wait(barrier, n_dp - 1 + n_mp - 1)
+    tab_c, fr_c, ct_c = [], [], []
+    for k in range(1, n_dp):
+        c = send(tables.at[me], tables.at[me], tab_s.at[k], tab_r.at[k], dp=dp_peer(k))
+        c.start()
+        tab_c.append(c)
+    for k in range(1, n_dp):
+        c = send(slots.at[dp_peer(k)], got.at[me], fr_s.at[k], fr_r.at[k], dp=dp_peer(k))
+        c.start()
+        fr_c.append(c)
+    for k in range(1, n_mp):
+        c = send(cot, cot_all.at[mine], ct_s.at[k], ct_r.at[k], mp=mp_peer(k))
+        c.start()
+        ct_c.append(c)
+
+    taps[0:KERNEL] = w_depth[...].astype(f32)
+    for ref in (hpad, gpad):
+        ref[0:pad] = jnp.zeros((pad, width), f32)
+        ref[pad + ROWS :] = jnp.zeros((pad, width), f32)
+    gfull[...] = jnp.zeros_like(gfull)
+
+    def arrived(dst, ssem, rsem, **where):
+        send(dst, dst, ssem, rsem, **where).wait_recv()
+
+    for k in range(1, n_dp):
+        src = dp_from(k)
+        arrived(tables.at[src], tab_s.at[k], tab_r.at[k], dp=src)
+
+    here = me.astype(f32)
+    t_row = lax.broadcasted_iota(jnp.int32, (ROWS, 1), 0).astype(f32)
+    lane = lax.broadcasted_iota(jnp.int32, (1, entries), 1).astype(f32)
+    shift = jnp.zeros((ROWS, entries), f32)
+    order = jnp.zeros((ROWS, entries), f32)
+    label = jnp.zeros((ROWS, entries), f32)
+    rank = jnp.zeros((1, 1), f32)
+    selectors = []
+    for s in range(n_dp):
+        table = tables[s]
+        t_len, t_dest, t_off, t_begin = table[0:1], table[1:2], table[2:3], table[3:4]
+        to_me = (t_dest == here) & (t_len > 0.0)
+        valid = jnp.max(jnp.where(to_me, 1.0, 0.0), axis=1, keepdims=True)
+        match = to_me & (t_off <= t_row) & (t_row < t_off + t_len)
+        inside = t_begin - slot_rows * jnp.floor(t_begin / slot_rows)
+        shift = shift + jnp.where(match, inside - t_off, 0.0)
+        order = order + jnp.where(match, rank, 0.0)
+        label = label + jnp.where(match, s * entries + lane, 0.0)
+        selectors.append([jnp.where((valid > 0.0) & (rank == r), 1.0, 0.0) for r in range(sources)])
+        rank = rank + valid
+    q = jnp.sum(shift, axis=1, keepdims=True) + t_row
+    rank_of = jnp.sum(order, axis=1, keepdims=True)
+    q_part = jnp.floor(q / quarter)
+    place = q_part * (sources * quarter) + rank_of * quarter + (q - q_part * quarter)
+    spots = lax.broadcasted_iota(jnp.int32, (ROWS, ROWS), 1).astype(f32)
+    pick_rows = jnp.where(spots == place, 1.0, 0.0).astype(bf16)
+    lab_pad[0:pad] = jnp.full((pad, 128), -1.0, f32)
+    lab_pad[pad + ROWS :] = jnp.full((pad, 128), -1.0, f32)
+    lab_pad[pad : pad + ROWS] = jnp.broadcast_to(jnp.sum(label, axis=1, keepdims=True), (ROWS, 128))
+    for j in range(KERNEL):
+        start = pad + j - centre
+        masks[j] = jnp.where(lab_pad[start : start + ROWS] == lab_pad[pad : pad + ROWS], 1.0, 0.0)
+
+    for k in range(1, n_dp):
+        src = dp_from(k)
+        arrived(got.at[src], fr_s.at[k], fr_r.at[k], dp=src)
+    picked = [jnp.zeros((quarter, features), f32) for _ in range(sources)]
+    for s in range(n_dp):
+        rows_s = got[s].astype(f32)
+        for r in range(sources):
+            picked[r] = picked[r] + selectors[s][r] * rows_s
+    comp_all[mine] = jnp.concatenate(picked, 0).astype(bf16)
+    cp_c = []
+    for k in range(1, n_mp):
+        c = send(comp_all.at[mine], comp_all.at[mine], cp_s.at[k], cp_r.at[k], mp=mp_peer(k))
+        c.start()
+        cp_c.append(c)
+
+    for k in range(1, n_mp):
+        src = mp_from(k)
+        arrived(cot_all.at[src], ct_s.at[k], ct_r.at[k], mp=src)
+    for b in range(n_mp):
+        cot_t[b * width : (b + 1) * width] = cot_all[b].T
+    for b in range(n_mp):
+        term = jnp.dot(cot_all[b], w_out[b * width : (b + 1) * width], preferred_element_type=f32)
+        gact[...] = term if b == 0 else gact[...] + term
+
+    for k in range(1, n_mp):
+        src = mp_from(k)
+        arrived(comp_all.at[src], cp_s.at[k], cp_r.at[k], mp=src)
+    everything = jnp.concatenate([comp_all[b] for b in range(n_mp)], 0)
+    packed[...] = jnp.dot(pick_rows, everything, preferred_element_type=f32).astype(bf16)
+    hpad[pad : pad + ROWS] = jnp.dot(packed[...], w_in[...], preferred_element_type=f32).astype(bf16).astype(f32)
+
+    def columns(c):
+        return pl.ds(pl.multiple_of(c * 128, 128), 128)
+
+    def conv(values, direction, emit):
+        def body(c, carry):
+            cs = columns(c)
+            weights = taps[:, cs]
+            for base in range(0, ROWS, chunk):
+                total = jnp.zeros((chunk, 128), f32)
+                for j in range(KERNEL):
+                    start = pad + base + direction * (j - centre)
+                    mask = masks[j if direction == 1 else KERNEL - 1 - j, base : base + chunk]
+                    total = total + weights[j : j + 1] * (values[start : start + chunk, cs] * mask)
+                emit(base, cs, total)
+            return carry
+
+        lax.fori_loop(0, width // 128, body, 0)
+
+    def forward(base, cs, total):
+        rows = slice(base, base + chunk)
+        gate = 1.0 / (1.0 + jnp.exp(-total))
+        act[rows, cs] = (total * gate).astype(bf16)
+        gpad[pad + base : pad + base + chunk, cs] = gact[rows, cs] * gate * (1.0 + total * (1.0 - gate))
+
+    conv(hpad, 1, forward)
+
+    def dw_rows(d):
+        at = pl.ds(pl.multiple_of(d * block, 64), block)
+        return jnp.dot(cot_t[at], act[...], preferred_element_type=f32)
+
+    z_order = [2, 1, 3, 0] if n_z == 4 else list(range(1, n_z)) + [0]
+    dy_c, dz_c, pt_c = [], [], []
+    for kz in z_order:
+        zt = lax.rem(zi + kz, n_z)
+        dy_send[kz] = dw_rows(2 * zt + 1 - yi).astype(bf16)
+        c = send(dy_send.at[kz], dy_got.at[kz], dy_s.at[kz], dy_r.at[kz], dp=2 * zi + 1 - yi)
+        c.start()
+        dy_c.append(c)
+    for k in [2, 3, 1, 0] if n_mp == 4 else list(range(1, n_mp)) + [0]:
+        at = pl.ds(pl.multiple_of(mp_peer(k) * width, 128), width)
+        part[k] = lax.dot_general(
+            act[...], w_out[at], (((1,), (1,)), ((), ())), preferred_element_type=f32
+        ).astype(bf16)
+        if k:
+            c = send(part.at[k], part_got.at[k], pt_s.at[k], pt_r.at[k], mp=mp_peer(k))
+            c.start()
+            pt_c.append(c)
+
+    def tap_body(c, carry):
+        cs = columns(c)
+        for j in range(KERNEL):
+            total = jnp.zeros((chunk, 128), f32)
+            for base in range(0, ROWS, chunk):
+                start = pad + base + j - centre
+                total = total + gpad[pad + base : pad + base + chunk, cs] * (
+                    hpad[start : start + chunk, cs] * masks[j, base : base + chunk]
+                )
+            gfull[features + j : features + j + 1, cs] = jnp.sum(total, axis=0, keepdims=True)
+        return carry
+
+    def backward(base, cs, total):
+        rows = slice(base, base + chunk)
+        ghid[rows, cs] = (cot[rows, cs].astype(f32) + total).astype(bf16)
+
+    def dz_step(kz):
+        zt = lax.rem(zi + kz, n_z)
+        arrived(dy_got.at[kz], dy_s.at[kz], dy_r.at[kz], dp=2 * zi + 1 - yi)
+        total = dw_rows(2 * zt + yi) + dy_got[kz].astype(f32)
+        if kz:
+            dz_send[kz] = total.astype(bf16)
+            c = send(dz_send.at[kz], dz_got.at[kz], dz_s.at[kz], dz_r.at[kz], dp=2 * zt + yi)
+            c.start()
+            dz_c.append(c)
+        else:
+            dz_own[...] = total
+
+    conv(gpad, -1, backward)
+    dz_step(z_order[0])
+    lax.fori_loop(0, width // 128, tap_body, 0)
+    gfull[0:features] = lax.dot_general(
+        packed[...], ghid[...], (((0,), (0,)), ((), ())), preferred_element_type=f32
+    )
+    for d in range(n_dp):
+        gs[d] = gfull[d * strip : (d + 1) * strip].astype(bf16)
+    gr_c, ga_c = [], []
+    for k in range(1, n_dp):
+        c = send(gs.at[dp_peer(k)], ggot.at[k], gr_s.at[k], gr_r.at[k], dp=dp_peer(k))
+        c.start()
+        gr_c.append(c)
+    for kz in z_order[1:]:
+        dz_step(kz)
+    total = gfull[pl.ds(pl.multiple_of(me * strip, 16), strip)]
+    for k in range(1, n_dp):
+        arrived(ggot.at[k], gr_s.at[k], gr_r.at[k], dp=dp_from(k))
+        total = total + ggot[k].astype(f32)
+    gall[me] = total.astype(bf16)
+    for k in range(1, n_dp):
+        c = send(gall.at[me], gall.at[me], ga_s.at[k], ga_r.at[k], dp=dp_peer(k))
+        c.start()
+        ga_c.append(c)
+
+    branch = part[0].astype(f32)
+    for k in range(1, n_mp):
+        arrived(part_got.at[k], pt_s.at[k], pt_r.at[k], mp=mp_from(k))
+        branch = branch + part_got[k].astype(f32)
+    out_ref[...] = (hpad[pad : pad + ROWS] + branch).astype(out_ref.dtype)
+    total = dz_own[...]
+    for kz in range(1, n_z):
+        src = 2 * lax.rem(zi + n_z - kz, n_z) + yi
+        arrived(dz_got.at[kz], dz_s.at[kz], dz_r.at[kz], dp=src)
+        total = total + dz_got[kz].astype(f32)
+    gout_ref[...] = scale * total
+    for k in range(1, n_dp):
+        src = dp_from(k)
+        arrived(gall.at[src], ga_s.at[k], ga_r.at[k], dp=src)
+    sums = scale * jnp.concatenate([gall[d].astype(f32) for d in range(n_dp)], 0)
+    gin_ref[...] = sums[0:features]
+    gdep_ref[...] = sums[features : features + KERNEL]
+    for c in tab_c + fr_c + ct_c + cp_c + dy_c + pt_c + dz_c + gr_c + ga_c:
+        c.wait_send()
+
+
+def fused(frames, lengths, destinations, offsets, in_weight, depth_weight, out_weight, cotangent):
+    n_dp, n_mp = lax.axis_size("dp"), lax.axis_size("mp")
+    src_rows, features = frames.shape
+    entries = lengths.shape[1]
+    width = cotangent.shape[1]
+    model = out_weight.shape[0]
+    block = model // n_dp
+    quarter = src_rows // n_dp // n_mp
+    sources = ROWS * n_dp // src_rows
+    strip = -(-(features + KERNEL) // (16 * n_dp)) * 16
+    n_z = n_dp // 2
+    f32, bf16 = jnp.float32, jnp.bfloat16
+    vm = pltpu.VMEM
+    scratch = [
+        vm((n_dp, 8, entries), f32),
+        vm((n_dp, quarter, features), bf16),
+        vm((n_dp, quarter, features), bf16),
+        vm((n_mp, sources * quarter, features), bf16),
+        vm((n_mp, ROWS, width), bf16),
+        vm((model, ROWS), bf16),
+        vm((ROWS, features), bf16),
+        vm((ROWS + 32, 128), f32),
+        vm((KERNEL, ROWS, 128), f32),
+        vm((32, width), f32),
+        vm((ROWS + 32, width), f32),
+        vm((ROWS, width), bf16),
+        vm((ROWS, width), f32),
+        vm((ROWS + 32, width), f32),
+        vm((ROWS, width), bf16),
+        vm((n_mp, ROWS, width), bf16),
+        vm((n_mp, ROWS, width), bf16),
+        vm((n_z, block, width), bf16),
+        vm((n_z, block, width), bf16),
+        vm((n_z, block, width), bf16),
+        vm((n_z, block, width), bf16),
+        vm((block, width), f32),
+        vm((n_dp * strip, width), f32),
+        vm((n_dp, strip, width), bf16),
+        vm((n_dp, strip, width), bf16),
+        vm((n_dp, strip, width), bf16),
+    ]
+    for count in (n_dp, n_dp, n_mp, n_mp, n_mp, n_z, n_z, n_dp, n_dp):
+        scratch += [pltpu.SemaphoreType.DMA((count,)), pltpu.SemaphoreType.DMA((count,))]
+    whole = pl.BlockSpec(memory_space=pltpu.VMEM)
+    return pl.pallas_call(
+        functools.partial(fused_kernel, n_dp, n_mp, 1.0 / math.sqrt(n_dp * ROWS)),
+        out_shape=(
+            jax.ShapeDtypeStruct((ROWS, width), bf16),
+            jax.ShapeDtypeStruct((features, width), f32),
+            jax.ShapeDtypeStruct((KERNEL, width), f32),
+            jax.ShapeDtypeStruct((block, width), f32),
+        ),
+        in_specs=[whole] * 8,
+        out_specs=(whole,) * 4,
+        scratch_shapes=scratch,
+        compiler_params=pltpu.CompilerParams(
+            collective_id=0, has_side_effects=True, vmem_limit_bytes=48 * 1024 * 1024
+        ),
+    )(frames, lengths, destinations, offsets, in_weight, depth_weight, out_weight, cotangent)
+
+
 def solution(mesh):
+    small = mesh.shape["dp"] <= 16 and mesh.shape["dp"] % 2 == 0
     placed = (
         P("dp", None),
         P("dp", None),
@@ -143,7 +495,7 @@
         P("dp", "mp"),
     )
     return jax.shard_map(
-        per_device,
+        fused if small else per_device,
         mesh=mesh,
         in_specs=placed,
         out_specs=(P("dp", "mp"), P(None, "mp"), P(None, "mp"), P("dp", "mp")),

time: 262 us -> 60.4 us (0.23)
  waiting for transfers between devices: 122 us -> 0 us
  Pallas kernels: 0 us -> 53.4 us
  blocking collectives: 46.8 us -> 0 us
  local copies, waits for them, and re-layouts: 36.8 us -> 6.02 us
  starting transfers between devices: 17.9 us -> 0 us
  between operations: 15.7 us -> 0.74 us
  other arithmetic: 11.4 us -> 0 us
  matrix products: 10.5 us -> 0 us
    unnamed x5 -> x0, waiting for transfers between devices: 86.3 us -> none
    pallas_call x0 -> x1, Pallas kernels: none -> 53.4 us  [fused(): pl.pallas_call(functools.partial(fused_kernel, n_dp, n_mp, 1.0 / math.sqr...]
    psum x1 -> x0, blocking collectives: 38.2 us -> none  [per_device(): in_weight_gradient, depth_gradient = lax.psum((term_in, term_depth), 'dp')]
    psum x1 -> x0, waiting for transfers between devices: 24.4 us -> none  [per_device(): in_weight_gradient, depth_gradient = lax.psum((term_in, term_depth), 'dp')]
    scatter x5 -> x0, local copies, waits for them, and re-layouts: 23.2 us -> none  [the longest x1 5.19 us: per_device(): send_frames = jnp.zeros((dump_index + 1, features), frames.dtype).at[slot...]
    all_to_all x3 -> x0, starting transfers between devices: 17.8 us -> none  [the longest x1 7.28 us: per_device(): lax.all_to_all(send_target, 'dp', split_axis=0, concat_axis=0, tiled=True)]
    all_to_all x3 -> x0, waiting for transfers between devices: 11.4 us -> none  [the longest x1 9.89 us: per_device(): lax.all_to_all(send_frames, 'dp', split_axis=0, concat_axis=0, tiled=True)]
    dot_general x5 -> x0, matrix products: 10.5 us -> none  [the longest x1 4.16 us: per_device(): lax.dot_general(packed, grad_hidden, (((0,), (0,)), ((), ())), preferred_...]
  transfers between devices with their start and end apart: 6 -> 0, of which waited for: 5 -> 0; matrix products, arithmetic and copies ran while one was open for 10% -> 0% of each run, Pallas kernels for 0% -> 0%
where the time goes in v1:
time: 60.4 us; the launch traced here: 60.1 us
  Pallas kernels  53.4 us (88%)
  local copies, waits for them, and re-layouts  6.02 us (10%)
  between operations  0.74 us (1%)
    pallas_call x1, Pallas kernels, fused(): pl.pallas_call(functools.partial(fused_kernel, n_dp, n_mp, 1.0 / math.sqr...  53.4 us
    unnamed x19, local copies, waits for them, and re-layouts  6.02 us

profile of v1, /device:TPU:0, one launch (start us, length us, event | category | flops | bytes accessed | tf_op | source)
XLA Modules:
  0.0 60.1 jit_solution(7072564384015713917)
XLA Ops:
  0.6 0.0 copy-start
  0.6 0.0 copy-start.1
  0.7 0.0 copy-start.6
  0.7 0.0 copy-start.5
  0.7 0.0 copy-start.4
  0.7 1.6 %copy.12.frames = bf16[1024,320]{1,0:T(8,128)(2,1)S(1)} copy(bf16[1024,320]{0,1:T(8,128)(2,1)} %param.8) | data formatting | bytes 1310720 | tf_op args[0]
  2.2 0.0 copy-done
  2.3 0.0 copy-done.1
  2.3 0.0 copy-done.6
  2.3 0.0 copy-done.5
  2.3 0.0 copy-done.4
  2.3 0.0 copy-start.2
  2.3 0.9 %copy-done.2 = bf16[256,384]{1,0:T(8,128)(2,1)S(1)} copy-done((bf16[256,384]{1,0:T(8,128)(2,1)S(1)}, bf16[256,384]{1,0:T(8,128)(2,1)}, u32[]{:S(2)}) %copy-start.2) | copy-done | bytes 196632
  3.2 0.0 copy-start.3
  3.2 0.7 %copy-done.3 = bf16[31,384]{1,0:T(8,128)(2,1)S(1)} copy-done((bf16[31,384]{1,0:T(8,128)(2,1)S(1)}, bf16[31,384]{1,0:T(8,128)(2,1)}, u32[]{:S(2)}) %copy-start.3) | copy-done | bytes 23832
  4.0 53.4 %shard_map.111 = (bf16[256,384]{1,0:T(8,128)(2,1)S(1)}, f32[320,384]{1,0:T(8,128)S(1)}, f32[31,384]{1,0:T(8,128)S(1)}, f32[192,384]{1,0:T(8,128)S(1)}) custom-call(bf16[1024,320]{1,0:T(8,128)(2,1)S(1)} %copy.12.frames, s32[1,128]{1,0:T(1,128)S(1)} %copy-done.4, s32[1,128]{1,0:T(1,128)S(1)} %copy-done.5, s32[1,128]{1,0:T(1,128)S(1)} %copy-done.6, ...), custom_call_target="tpu_custom_call" | custom-call | tf_op jit(solution)/shard_map/pallas_call | solution.py:468
  57.3 0.7 %copy.17 = bf16[256,384]{1,0:T(8,128)(2,1)} copy(bf16[256,384]{1,0:T(8,128)(2,1)S(1)} %get-tuple-element.8) | data formatting | bytes 393216
  58.0 0.8 %copy.18 = f32[320,384]{1,0:T(8,128)} copy(f32[320,384]{1,0:T(8,128)S(1)} %get-tuple-element.9) | data formatting | bytes 983040
  58.8 0.6 %copy.19 = f32[31,384]{1,0:T(8,128)} copy(f32[31,384]{1,0:T(8,128)S(1)} %get-tuple-element.10) | data formatting | bytes 95232
  59.4 0.7 %copy.20 = f32[192,384]{1,0:T(8,128)} copy(f32[192,384]{1,0:T(8,128)S(1)} %get-tuple-element.11) | data formatting | bytes 589824
Async XLA Ops:
  0.6 1.6 %copy-start = (bf16[1536,384]{1,0:T(8,128)(2,1)S(1)}, bf16[1536,384]{1,0:T(8,128)(2,1)}, u32[]{:S(2)}) copy-start(bf16[1536,384]{1,0:T(8,128)(2,1)} %w_out.1) | copy-start | bytes 3538948
  0.6 1.6 %copy-start.1 = (bf16[320,384]{1,0:T(8,128)(2,1)S(1)}, bf16[320,384]{1,0:T(8,128)(2,1)}, u32[]{:S(2)}) copy-start(bf16[320,384]{1,0:T(8,128)(2,1)} %w_in.1) | copy-start | bytes 737284
  0.7 1.6 %copy-start.6 = (s32[1,128]{1,0:T(1,128)S(1)}, s32[1,128]{1,0:T(1,128)}, u32[]{:S(2)}) copy-start(s32[1,128]{1,0:T(1,128)} %offs.1) | copy-start | bytes 1540
  0.7 1.6 %copy-start.5 = (s32[1,128]{1,0:T(1,128)S(1)}, s32[1,128]{1,0:T(1,128)}, u32[]{:S(2)}) copy-start(s32[1,128]{1,0:T(1,128)} %dests.1) | copy-start | bytes 1540
  0.7 1.6 %copy-start.4 = (s32[1,128]{1,0:T(1,128)S(1)}, s32[1,128]{1,0:T(1,128)}, u32[]{:S(2)}) copy-start(s32[1,128]{1,0:T(1,128)} %lens.1) | copy-start | bytes 1540
  2.3 0.9 %copy-start.2 = (bf16[256,384]{1,0:T(8,128)(2,1)S(1)}, bf16[256,384]{1,0:T(8,128)(2,1)}, u32[]{:S(2)}) copy-start(bf16[256,384]{1,0:T(8,128)(2,1)} %cot.1) | copy-start | bytes 589828
  3.2 0.7 %copy-start.3 = (bf16[31,384]{1,0:T(8,128)(2,1)S(1)}, bf16[31,384]{1,0:T(8,128)(2,1)}, u32[]{:S(2)}) copy-start(bf16[31,384]{1,0:T(8,128)(2,1)} %w_depth.1) | copy-start | bytes 71428

commit v2 on v1

--- a/solution.py
+++ b/solution.py
@@ -137,23 +137,24 @@
 
 def fused_kernel(
     n_dp, n_mp, scale,
-    frames, lens, dests, offs, w_in, w_depth, w_out, cot,
+    frames_in, lens_in, dests_in, offs_in, w_in_in, w_depth_in, w_out_in, cot_in,
     out_ref, gin_ref, gdep_ref, gout_ref,
+    frames, lens, dests, offs, w_in, w_depth, w_out, in_sem,
     tables, slots, got, comp_all, cot_all, cot_t, packed, lab_pad, masks, taps, hpad, act, gact, gpad, ghid,
-    part, part_got, dy_send, dy_got, dz_send, dz_got, dz_own, gfull, gs, ggot, gall,
-    tab_s, tab_r, fr_s, fr_r, cp_s, cp_r, ct_s, ct_r, pt_s, pt_r, dy_s, dy_r, dz_s, dz_r, gr_s, gr_r, ga_s, ga_r,
+    part, part_got, dy_send, dy_got, dz_send, dz_got, dz_own, gfull, tap_acc, gs, gy_got, gz_send, gz_got, gall,
+    tab_s, tab_r, fr_s, fr_r, cp_s, cp_r, ct_s, ct_r, pt_s, pt_r, dy_s, dy_r, dz_s, dz_r, gy_s, gy_r, gz_s, gz_r, ga_s, ga_r, gb_s, gb_r,
 ):
     f32, bf16 = jnp.float32, jnp.bfloat16
     me = lax.axis_index("dp")
     mine = lax.axis_index("mp")
-    src_rows, features = frames.shape
+    features, src_rows = frames.shape
     slot_rows = src_rows // n_dp
     quarter = slot_rows // n_mp
     sources = ROWS // slot_rows
-    width = cot.shape[1]
+    width = cot_all.shape[2]
     entries = lens.shape[1]
     block = gout_ref.shape[0]
-    strip = gs.shape[1]
+    strip = gs.shape[2]
     centre = (KERNEL - 1) // 2
     pad = 16
     n_z = n_dp // 2
@@ -177,12 +178,23 @@
             src_ref=src, dst_ref=dst, send_sem=ssem, recv_sem=rsem, device_id=where, device_id_type=MESH
         )
 
+    loads = [
+        pltpu.make_async_copy(src, dst, in_sem.at[i])
+        for i, (src, dst) in enumerate(
+            [(lens_in, lens), (dests_in, dests), (offs_in, offs), (frames_in, frames), (cot_in, cot_all.at[mine]),
+             (w_depth_in, w_depth), (w_in_in, w_in), (w_out_in, w_out)]
+        )
+    ]
+    for load in loads:
+        load.start()
     barrier = pltpu.get_barrier_semaphore()
     for k in range(1, n_dp):
         pl.semaphore_signal(barrier, inc=1, device_id={"dp": dp_peer(k)}, device_id_type=MESH)
     for k in range(1, n_mp):
         pl.semaphore_signal(barrier, inc=1, device_id={"mp": mp_peer(k)}, device_id_type=MESH)
 
+    for load in loads[:3]:
+        load.wait()
     len_f = lens[...].astype(f32)
     dest_f = dests[...].astype(f32)
     off_f = offs[...].astype(f32)
@@ -201,11 +213,13 @@
     wanted = first + row_in + (mine * quarter).astype(f32)
     cols = lax.broadcasted_iota(jnp.int32, (n_dp * quarter, src_rows), 1).astype(f32)
     pick = jnp.where(cols == wanted, 1.0, 0.0).astype(bf16)
-    chosen = jnp.dot(pick, frames[...], preferred_element_type=f32).astype(bf16)
+    loads[3].wait()
+    chosen = lax.dot_general(
+        pick, frames[...], (((1,), (1,)), ((), ())), preferred_element_type=f32
+    ).astype(bf16)
     for d in range(n_dp):
         slots[d] = chosen[d * quarter : (d + 1) * quarter]
     got[me] = slots[me]
-    cot_all[mine] = cot[...]
 
     pl.semaphore_wait(barrier, n_dp - 1 + n_mp - 1)
     tab_c, fr_c, ct_c = [], [], []
@@ -217,10 +231,14 @@
         c = send(slots.at[dp_peer(k)], got.at[me], fr_s.at[k], fr_r.at[k], dp=dp_peer(k))
         c.start()
         fr_c.append(c)
-    for k in range(1, n_mp):
-        c = send(cot, cot_all.at[mine], ct_s.at[k], ct_r.at[k], mp=mp_peer(k))
+    sibling = mine + 1 - 2 * lax.rem(mine, 2)
+    across = lax.rem(mine + 2, n_mp)
+    for k, peer in ((0, across), (1, sibling)):
+        c = send(cot_in, cot_all.at[mine], ct_s.at[k], ct_r.at[k], mp=peer)
         c.start()
         ct_c.append(c)
+    for load in loads[4:]:
+        load.wait()
 
     taps[0:KERNEL] = w_depth[...].astype(f32)
     for ref in (hpad, gpad):
@@ -283,14 +301,25 @@
         c.start()
         cp_c.append(c)
 
-    for k in range(1, n_mp):
-        src = mp_from(k)
-        arrived(cot_all.at[src], ct_s.at[k], ct_r.at[k], mp=src)
-    for b in range(n_mp):
-        cot_t[b * width : (b + 1) * width] = cot_all[b].T
-    for b in range(n_mp):
-        term = jnp.dot(cot_all[b], w_out[b * width : (b + 1) * width], preferred_element_type=f32)
-        gact[...] = term if b == 0 else gact[...] + term
+    arrived(cot_all.at[across], ct_s.at[0], ct_r.at[0], mp=across)
+    c = send(cot_all.at[across], cot_all.at[across], ct_s.at[2], ct_r.at[2], mp=sibling)
+    c.start()
+    ct_c.append(c)
+
+    def use_cotangent(b, start):
+        at = pl.ds(pl.multiple_of(b * width, 128), width)
+        values = cot_all[b]
+        cot_t[at] = values.T
+        term = jnp.dot(values, w_out[at], preferred_element_type=f32)
+        gact[...] = term if start else gact[...] + term
+
+    use_cotangent(mine, True)
+    use_cotangent(across, False)
+    arrived(cot_all.at[sibling], ct_s.at[1], ct_r.at[1], mp=sibling)
+    use_cotangent(sibling, False)
+    diagonal = lax.rem(sibling + 2, n_mp)
+    arrived(cot_all.at[diagonal], ct_s.at[2], ct_r.at[2], mp=sibling)
+    use_cotangent(diagonal, False)
 
     for k in range(1, n_mp):
         src = mp_from(k)
@@ -330,14 +359,31 @@
         return jnp.dot(cot_t[at], act[...], preferred_element_type=f32)
 
     z_order = [2, 1, 3, 0] if n_z == 4 else list(range(1, n_z)) + [0]
+    partner = 2 * zi + 1 - yi
     dy_c, dz_c, pt_c = [], [], []
-    for kz in z_order:
+
+    def dy_step(kz):
         zt = lax.rem(zi + kz, n_z)
         dy_send[kz] = dw_rows(2 * zt + 1 - yi).astype(bf16)
-        c = send(dy_send.at[kz], dy_got.at[kz], dy_s.at[kz], dy_r.at[kz], dp=2 * zi + 1 - yi)
+        c = send(dy_send.at[kz], dy_got.at[kz], dy_s.at[kz], dy_r.at[kz], dp=partner)
         c.start()
         dy_c.append(c)
-    for k in [2, 3, 1, 0] if n_mp == 4 else list(range(1, n_mp)) + [0]:
+
+    def dz_step(kz):
+        zt = lax.rem(zi + kz, n_z)
+        arrived(dy_got.at[kz], dy_s.at[kz], dy_r.at[kz], dp=partner)
+        total = dw_rows(2 * zt + yi) + dy_got[kz].astype(f32)
+        if kz:
+            dz_send[kz] = total.astype(bf16)
+            c = send(dz_send.at[kz], dz_got.at[kz], dz_s.at[kz], dz_r.at[kz], dp=2 * zt + yi)
+            c.start()
+            dz_c.append(c)
+        else:
+            dz_own[...] = total
+
+    for kz in z_order[:-2]:
+        dy_step(kz)
+    for k in [2, 3, 1, 0]:
         at = pl.ds(pl.multiple_of(mp_peer(k) * width, 128), width)
         part[k] = lax.dot_general(
             act[...], w_out[at], (((1,), (1,)), ((), ())), preferred_element_type=f32
@@ -347,78 +393,105 @@
             c.start()
             pt_c.append(c)
 
-    def tap_body(c, carry):
+    def backward(c, carry):
         cs = columns(c)
+        weights = taps[:, cs]
+        for base in range(0, ROWS, chunk):
+            rows = slice(base, base + chunk)
+            values = hpad[pad + base : pad + base + chunk, cs]
+            total = cot_all[mine, rows, cs].astype(f32)
+            for j in range(KERNEL):
+                start = pad + base - (j - centre)
+                taken = gpad[start : start + chunk, cs] * masks[KERNEL - 1 - j, rows]
+                total = total + weights[j : j + 1] * taken
+                sums = jnp.sum((values * taken).reshape(chunk // 8, 8, 128), axis=0)
+                tap_acc[j] = sums if base == 0 else tap_acc[j] + sums
+            ghid[rows, cs] = total.astype(bf16)
         for j in range(KERNEL):
-            total = jnp.zeros((chunk, 128), f32)
-            for base in range(0, ROWS, chunk):
-                start = pad + base + j - centre
-                total = total + gpad[pad + base : pad + base + chunk, cs] * (
-                    hpad[start : start + chunk, cs] * masks[j, base : base + chunk]
-                )
-            gfull[features + j : features + j + 1, cs] = jnp.sum(total, axis=0, keepdims=True)
+            gfull[features + j : features + j + 1, cs] = jnp.sum(tap_acc[j], axis=0, keepdims=True)
         return carry
 
-    def backward(base, cs, total):
-        rows = slice(base, base + chunk)
-        ghid[rows, cs] = (cot[rows, cs].astype(f32) + total).astype(bf16)
-
-    def dz_step(kz):
-        zt = lax.rem(zi + kz, n_z)
-        arrived(dy_got.at[kz], dy_s.at[kz], dy_r.at[kz], dp=2 * zi + 1 - yi)
-        total = dw_rows(2 * zt + yi) + dy_got[kz].astype(f32)
-        if kz:
-            dz_send[kz] = total.astype(bf16)
-            c = send(dz_send.at[kz], dz_got.at[kz], dz_s.at[kz], dz_r.at[kz], dp=2 * zt + yi)
-            c.start()
-            dz_c.append(c)
-        else:
-            dz_own[...] = total
-
-    conv(gpad, -1, backward)
+    tiles = width // 128
+    lax.fori_loop(0, tiles - 1, backward, 0)
     dz_step(z_order[0])
-    lax.fori_loop(0, width // 128, tap_body, 0)
+    lax.fori_loop(tiles - 1, tiles, backward, 0)
     gfull[0:features] = lax.dot_general(
         packed[...], ghid[...], (((0,), (0,)), ((), ())), preferred_element_type=f32
     )
-    for d in range(n_dp):
-        gs[d] = gfull[d * strip : (d + 1) * strip].astype(bf16)
-    gr_c, ga_c = [], []
-    for k in range(1, n_dp):
-        c = send(gs.at[dp_peer(k)], ggot.at[k], gr_s.at[k], gr_r.at[k], dp=dp_peer(k))
-        c.start()
-        gr_c.append(c)
-    for kz in z_order[1:]:
+    for y in range(2):
+        for z in range(n_z):
+            at = (y * n_z + z) * strip
+            gs[y, z] = gfull[at : at + strip].astype(bf16)
+    g_c = []
+
+    def push(src, dst, ssem, rsem, peer):
+        c = send(src, dst, ssem, rsem, dp=peer)
+        c.start()
+        g_c.append(c)
+
+    push(gs.at[1 - yi], gy_got, gy_s.at[0], gy_r.at[0], partner)
+    for kz in z_order[-2:]:
+        dy_step(kz)
+    for kz in z_order[1:-2]:
         dz_step(kz)
-    total = gfull[pl.ds(pl.multiple_of(me * strip, 16), strip)]
-    for k in range(1, n_dp):
-        arrived(ggot.at[k], gr_s.at[k], gr_r.at[k], dp=dp_from(k))
-        total = total + ggot[k].astype(f32)
-    gall[me] = total.astype(bf16)
-    for k in range(1, n_dp):
-        c = send(gall.at[me], gall.at[me], ga_s.at[k], ga_r.at[k], dp=dp_peer(k))
-        c.start()
-        ga_c.append(c)
+    arrived(gy_got, gy_s.at[0], gy_r.at[0], dp=partner)
+    for kz in z_order:
+        zt = lax.rem(zi + kz, n_z)
+        at = pl.ds(pl.multiple_of((yi * n_z + zt) * strip, 16), strip)
+        total = gfull[at] + gy_got[zt].astype(f32)
+        if kz:
+            gz_send[kz] = total.astype(bf16)
+            push(gz_send.at[kz], gz_got.at[kz], gz_s.at[kz], gz_r.at[kz], 2 * zt + yi)
+    dz_step(z_order[-2])
+    for kz in range(1, n_z):
+        arrived(gz_got.at[kz], gz_s.at[kz], gz_r.at[kz], dp=2 * lax.rem(zi + n_z - kz, n_z) + yi)
+        total = total + gz_got[kz].astype(f32)
+    gall[yi, zi] = total.astype(bf16)
+    for kz in z_order[:-1]:
+        zt = lax.rem(zi + kz, n_z)
+        push(gall.at[yi, zi], gall.at[yi, zi], ga_s.at[kz], ga_r.at[kz], 2 * zt + yi)
+    push(gall.at[yi, zi], gall.at[yi, zi], gb_s.at[0], gb_r.at[0], partner)
+    dz_step(0)
 
     branch = part[0].astype(f32)
     for k in range(1, n_mp):
         arrived(part_got.at[k], pt_s.at[k], pt_r.at[k], mp=mp_from(k))
         branch = branch + part_got[k].astype(f32)
     out_ref[...] = (hpad[pad : pad + ROWS] + branch).astype(out_ref.dtype)
+    for kz in range(1, n_z):
+        src = lax.rem(zi + n_z - kz, n_z)
+        arrived(gall.at[yi, src], ga_s.at[kz], ga_r.at[kz], dp=2 * src + yi)
+        push(gall.at[yi, src], gall.at[yi, src], gb_s.at[kz], gb_r.at[kz], partner)
     total = dz_own[...]
     for kz in range(1, n_z):
         src = 2 * lax.rem(zi + n_z - kz, n_z) + yi
         arrived(dz_got.at[kz], dz_s.at[kz], dz_r.at[kz], dp=src)
         total = total + dz_got[kz].astype(f32)
     gout_ref[...] = scale * total
-    for k in range(1, n_dp):
-        src = dp_from(k)
-        arrived(gall.at[src], ga_s.at[k], ga_r.at[k], dp=src)
-    sums = scale * jnp.concatenate([gall[d].astype(f32) for d in range(n_dp)], 0)
-    gin_ref[...] = sums[0:features]
-    gdep_ref[...] = sums[features : features + KERNEL]
-    for c in tab_c + fr_c + ct_c + cp_c + dy_c + pt_c + dz_c + gr_c + ga_c:
+    for kz in range(n_z):
+        src = lax.rem(zi + n_z - kz, n_z)
+        arrived(gall.at[1 - yi, src], gb_s.at[kz], gb_r.at[kz], dp=partner)
+    for y in range(2):
+        for z in range(n_z):
+            at = (y * n_z + z) * strip
+            values = scale * gall[y, z].astype(f32)
+            low = min(max(features - at, 0), strip)
+            high = min(max(features + KERNEL - at, 0), strip)
+            if low > 0:
+                gin_ref[at : at + low] = values[:low]
+            if high > low:
+                gdep_ref[at + low - features : at + high - features] = values[low:high]
+    for c in tab_c + fr_c + ct_c + cp_c + dy_c + pt_c + dz_c + g_c:
         c.wait_send()
+
+
+def store_kernel(*refs):
+    count = len(refs) // 2
+    copies = [pltpu.make_async_copy(refs[i], refs[count + i], refs[-1].at[i]) for i in range(count)]
+    for c in copies:
+        c.start()
+    for c in copies:
+        c.wait()
 
 
 def fused(frames, lengths, destinations, offsets, in_weight, depth_weight, out_weight, cotangent):
@@ -434,7 +507,16 @@
     n_z = n_dp // 2
     f32, bf16 = jnp.float32, jnp.bfloat16
     vm = pltpu.VMEM
+    i32 = jnp.int32
     scratch = [
+        vm((features, src_rows), bf16),
+        vm((1, entries), i32),
+        vm((1, entries), i32),
+        vm((1, entries), i32),
+        vm((features, width), bf16),
+        vm((KERNEL, width), bf16),
+        vm((model, width), bf16),
+        pltpu.SemaphoreType.DMA((8,)),
         vm((n_dp, 8, entries), f32),
         vm((n_dp, quarter, features), bf16),
         vm((n_dp, quarter, features), bf16),
@@ -458,14 +540,18 @@
         vm((n_z, block, width), bf16),
         vm((block, width), f32),
         vm((n_dp * strip, width), f32),
-        vm((n_dp, strip, width), bf16),
-        vm((n_dp, strip, width), bf16),
-        vm((n_dp, strip, width), bf16),
+        vm((KERNEL, 8, 128), f32),
+        vm((2, n_z, strip, width), bf16),
+        vm((n_z, strip, width), bf16),
+        vm((n_z, strip, width), bf16),
+        vm((n_z, strip, width), bf16),
+        vm((2, n_z, strip, width), bf16),
     ]
-    for count in (n_dp, n_dp, n_mp, n_mp, n_mp, n_z, n_z, n_dp, n_dp):
+    for count in (n_dp, n_dp, n_mp, n_mp, n_mp, n_z, n_z, 1, n_z, n_z, n_z):
         scratch += [pltpu.SemaphoreType.DMA((count,)), pltpu.SemaphoreType.DMA((count,))]
     whole = pl.BlockSpec(memory_space=pltpu.VMEM)
-    return pl.pallas_call(
+    remote = pl.BlockSpec(memory_space=pltpu.HBM)
+    results = pl.pallas_call(
         functools.partial(fused_kernel, n_dp, n_mp, 1.0 / math.sqrt(n_dp * ROWS)),
         out_shape=(
             jax.ShapeDtypeStruct((ROWS, width), bf16),
@@ -473,17 +559,24 @@
             jax.ShapeDtypeStruct((KERNEL, width), f32),
             jax.ShapeDtypeStruct((block, width), f32),
         ),
-        in_specs=[whole] * 8,
+        in_specs=[remote] * 8,
         out_specs=(whole,) * 4,
         scratch_shapes=scratch,
         compiler_params=pltpu.CompilerParams(
             collective_id=0, has_side_effects=True, vmem_limit_bytes=48 * 1024 * 1024
         ),
-    )(frames, lengths, destinations, offsets, in_weight, depth_weight, out_weight, cotangent)
+    )(frames.T, lengths, destinations, offsets, in_weight, depth_weight, out_weight, cotangent)
+    return pl.pallas_call(
+        store_kernel,
+        out_shape=tuple(jax.ShapeDtypeStruct(r.shape, r.dtype) for r in results),
+        in_specs=[whole] * 4,
+        out_specs=(remote,) * 4,
+        scratch_shapes=[pltpu.SemaphoreType.DMA((4,))],
+    )(*results)
 
 
 def solution(mesh):
-    small = mesh.shape["dp"] <= 16 and mesh.shape["dp"] % 2 == 0
+    small = mesh.shape["dp"] == 8 and mesh.shape["mp"] == 4
     placed = (
         P("dp", None),
         P("dp", None),

time: 60.4 us -> 67.6 us (1.12)
  local copies, waits for them, and re-layouts: 6.02 us -> 9.7 us
  Pallas kernels: 53.4 us -> 56.9 us
    unnamed x19 -> x24, local copies, waits for them, and re-layouts: 6.02 us -> 9.7 us
    pallas_call x0 -> x1, Pallas kernels: none -> 2.21 us  [fused(): pl.pallas_call(store_kernel, out_shape=tuple((jax.ShapeDtypeStruct(r.shap...]
    pallas_call x1, Pallas kernels: 53.4 us -> 54.7 us  [fused(): pl.pallas_call(functools.partial(fused_kernel, n_dp, n_mp, 1.0 / math.sqr...]
where the time goes in v2:
time: 67.6 us; the launch traced here: 67.3 us
  Pallas kernels  56.9 us (84%)
  local copies, waits for them, and re-layouts  9.7 us (14%)
    pallas_call x1, Pallas kernels, fused(): pl.pallas_call(functools.partial(fused_kernel, n_dp, n_mp, 1.0 / math.sqr...  54.7 us
    unnamed x24, local copies, waits for them, and re-layouts  9.7 us
    pallas_call x1, Pallas kernels, fused(): pl.pallas_call(store_kernel, out_shape=tuple((jax.ShapeDtypeStruct(r.shap...  2.21 us

profile of v2, /device:TPU:0, one launch (start us, length us, event | category | flops | bytes accessed | tf_op | source)
XLA Modules:
  0.0 67.3 jit_solution(14461502878067418720)
XLA Ops:
  0.6 0.0 copy-start
  0.6 1.3 %copy-done = bf16[1536,384]{1,0:T(8,128)(2,1)S(1)} copy-done((bf16[1536,384]{1,0:T(8,128)(2,1)S(1)}, bf16[1536,384]{1,0:T(8,128)(2,1)}, u32[]{:S(2)}) %copy-start) | copy-done | bytes 1179672
  1.9 0.0 copy-start.1
  1.9 1.1 %copy-done.1 = bf16[1024,320]{0,1:T(8,128)(2,1)S(1)} copy-done((bf16[1024,320]{0,1:T(8,128)(2,1)S(1)}, bf16[1024,320]{0,1:T(8,128)(2,1)}, u32[]{:S(2)}) %copy-start.1) | copy-done | bytes 655384
  3.0 0.0 copy-start.4
  3.0 0.9 %copy-done.4 = bf16[320,384]{1,0:T(8,128)(2,1)S(1)} copy-done((bf16[320,384]{1,0:T(8,128)(2,1)S(1)}, bf16[320,384]{1,0:T(8,128)(2,1)}, u32[]{:S(2)}) %copy-start.4) | copy-done | bytes 245784
  3.9 0.0 copy-start.5
  3.9 0.9 %copy-done.5 = bf16[256,384]{1,0:T(8,128)(2,1)S(1)} copy-done((bf16[256,384]{1,0:T(8,128)(2,1)S(1)}, bf16[256,384]{1,0:T(8,128)(2,1)}, u32[]{:S(2)}) %copy-start.5) | copy-done | bytes 196632
  4.9 0.0 copy-start.8
  4.9 0.7 %copy-done.8 = bf16[31,384]{1,0:T(8,128)(2,1)S(1)} copy-done((bf16[31,384]{1,0:T(8,128)(2,1)S(1)}, bf16[31,384]{1,0:T(8,128)(2,1)}, u32[]{:S(2)}) %copy-start.8) | copy-done | bytes 23832
  5.6 0.0 copy-start.9
  5.6 0.7 copy-done.9
  6.3 0.0 copy-start.10
  6.3 0.7 copy-done.10
  6.9 0.0 copy-start.11
  6.9 0.7 copy-done.11
  7.6 54.7 %shard_map.111 = (bf16[256,384]{1,0:T(8,128)(2,1)S(1)}, f32[320,384]{1,0:T(8,128)S(1)}, f32[31,384]{1,0:T(8,128)S(1)}, f32[192,384]{1,0:T(8,128)S(1)}) custom-call(bf16[320,1024]{1,0:T(8,128)(2,1)S(1)} %bitcast.1, s32[1,128]{1,0:T(1,128)S(1)} %copy-done.9, s32[1,128]{1,0:T(1,128)S(1)} %copy-done.10, s32[1,128]{1,0:T(1,128)S(1)} %copy-done.11, ...), custom_call_target="tpu_custom_call" | custom-call | tf_op jit(solution)/shard_map/pallas_call | solution.py:554
  62.3 0.0 copy-start.2
  62.3 0.8 %copy-done.2 = f32[320,384]{1,0:T(8,128)} copy-done((f32[320,384]{1,0:T(8,128)}, f32[320,384]{1,0:T(8,128)S(1)}, u32[]{:S(2)}) %copy-start.2) | copy-done | bytes 491544
  63.1 0.0 copy-start.3
  63.1 0.7 %copy-done.3 = f32[192,384]{1,0:T(8,128)} copy-done((f32[192,384]{1,0:T(8,128)}, f32[192,384]{1,0:T(8,128)S(1)}, u32[]{:S(2)}) %copy-start.3) | copy-done | bytes 294936
  63.8 0.7 %copy-done.6 = bf16[256,384]{1,0:T(8,128)(2,1)} copy-done((bf16[256,384]{1,0:T(8,128)(2,1)}, bf16[256,384]{1,0:T(8,128)(2,1)S(1)}, u32[]{:S(2)}) %copy-start.6) | copy-done | bytes 196632
  64.4 0.6 copy-done.7
  65.1 2.2 %shard_map.112 = (bf16[256,384]{1,0:T(8,128)(2,1)}, f32[320,384]{1,0:T(8,128)}, f32[31,384]{1,0:T(8,128)}, f32[192,384]{1,0:T(8,128)}) custom-call(bf16[256,384]{1,0:T(8,128)(2,1)} %copy-done.6, f32[320,384]{1,0:T(8,128)} %copy-done.2, f32[31,384]{1,0:T(8,128)} %copy-done.7, f32[192,384]{1,0:T(8,128)} %copy-done.3), custom_call_target="tpu_custom_call" | custom-call | tf_op jit(solution)/shard_map/pallas_call | solution.py:569
  (2 shorter events, 0.0 us)
Async XLA Ops:
  0.6 1.3 %copy-start = (bf16[1536,384]{1,0:T(8,128)(2,1)S(1)}, bf16[1536,384]{1,0:T(8,128)(2,1)}, u32[]{:S(2)}) copy-start(bf16[1536,384]{1,0:T(8,128)(2,1)} %w_out_in.1) | copy-start | bytes 3538948
  1.9 1.1 %copy-start.1 = (bf16[1024,320]{0,1:T(8,128)(2,1)S(1)}, bf16[1024,320]{0,1:T(8,128)(2,1)}, u32[]{:S(2)}) copy-start(bf16[1024,320]{0,1:T(8,128)(2,1)} %param.8) | copy-start | bytes 1966084
  3.0 0.9 %copy-start.4 = (bf16[320,384]{1,0:T(8,128)(2,1)S(1)}, bf16[320,384]{1,0:T(8,128)(2,1)}, u32[]{:S(2)}) copy-start(bf16[320,384]{1,0:T(8,128)(2,1)} %w_in_in.1) | copy-start | bytes 737284
  3.9 0.9 %copy-start.5 = (bf16[256,384]{1,0:T(8,128)(2,1)S(1)}, bf16[256,384]{1,0:T(8,128)(2,1)}, u32[]{:S(2)}) copy-start(bf16[256,384]{1,0:T(8,128)(2,1)} %cot_in.1) | copy-start | bytes 589828
  4.9 0.7 %copy-start.8 = (bf16[31,384]{1,0:T(8,128)(2,1)S(1)}, bf16[31,384]{1,0:T(8,128)(2,1)}, u32[]{:S(2)}) copy-start(bf16[31,384]{1,0:T(8,128)(2,1)} %w_depth_in.1) | copy-start | bytes 71428
  5.6 0.7 copy-start.9
  6.3 0.7 copy-start.10
  6.9 0.7 copy-start.11
  62.3 0.8 %copy-start.2 = (f32[320,384]{1,0:T(8,128)}, f32[320,384]{1,0:T(8,128)S(1)}, u32[]{:S(2)}) copy-start(f32[320,384]{1,0:T(8,128)S(1)} %get-tuple-element.9.refs_1_) | copy-start | bytes 1474564
  63.1 0.7 %copy-start.3 = (f32[192,384]{1,0:T(8,128)}, f32[192,384]{1,0:T(8,128)S(1)}, u32[]{:S(2)}) copy-start(f32[192,384]{1,0:T(8,128)S(1)} %get-tuple-element.11.refs_3_) | copy-start | bytes 884740
  63.8 0.7 %copy-start.6 = (bf16[256,384]{1,0:T(8,128)(2,1)}, bf16[256,384]{1,0:T(8,128)(2,1)S(1)}, u32[]{:S(2)}) copy-start(bf16[256,384]{1,0:T(8,128)(2,1)S(1)} %get-tuple-element.8.refs_0_) | copy-start | bytes 589828
  64.4 0.6 copy-start.7

commit v3 on v2

--- a/solution.py
+++ b/solution.py
@@ -178,6 +178,7 @@
             src_ref=src, dst_ref=dst, send_sem=ssem, recv_sem=rsem, device_id=where, device_id_type=MESH
         )
 
+    tiles = width // 128
     loads = [
         pltpu.make_async_copy(src, dst, in_sem.at[i])
         for i, (src, dst) in enumerate(
@@ -242,8 +243,8 @@
 
     taps[0:KERNEL] = w_depth[...].astype(f32)
     for ref in (hpad, gpad):
-        ref[0:pad] = jnp.zeros((pad, width), f32)
-        ref[pad + ROWS :] = jnp.zeros((pad, width), f32)
+        ref[:, 0:pad] = jnp.zeros((tiles, pad, 128), f32)
+        ref[:, pad + ROWS :] = jnp.zeros((tiles, pad, 128), f32)
     gfull[...] = jnp.zeros_like(gfull)
 
     def arrived(dst, ssem, rsem, **where):
@@ -326,63 +327,60 @@
         arrived(comp_all.at[src], cp_s.at[k], cp_r.at[k], mp=src)
     everything = jnp.concatenate([comp_all[b] for b in range(n_mp)], 0)
     packed[...] = jnp.dot(pick_rows, everything, preferred_element_type=f32).astype(bf16)
-    hpad[pad : pad + ROWS] = jnp.dot(packed[...], w_in[...], preferred_element_type=f32).astype(bf16).astype(f32)
+    hidden = jnp.dot(packed[...], w_in[...], preferred_element_type=f32).astype(bf16).astype(f32)
+    for c in range(tiles):
+        hpad[c, pad : pad + ROWS] = hidden[:, c * 128 : (c + 1) * 128]
 
     def columns(c):
         return pl.ds(pl.multiple_of(c * 128, 128), 128)
 
-    def conv(values, direction, emit):
-        def body(c, carry):
-            cs = columns(c)
-            weights = taps[:, cs]
-            for base in range(0, ROWS, chunk):
-                total = jnp.zeros((chunk, 128), f32)
-                for j in range(KERNEL):
-                    start = pad + base + direction * (j - centre)
-                    mask = masks[j if direction == 1 else KERNEL - 1 - j, base : base + chunk]
-                    total = total + weights[j : j + 1] * (values[start : start + chunk, cs] * mask)
-                emit(base, cs, total)
-            return carry
-
-        lax.fori_loop(0, width // 128, body, 0)
-
-    def forward(base, cs, total):
-        rows = slice(base, base + chunk)
-        gate = 1.0 / (1.0 + jnp.exp(-total))
-        act[rows, cs] = (total * gate).astype(bf16)
-        gpad[pad + base : pad + base + chunk, cs] = gact[rows, cs] * gate * (1.0 + total * (1.0 - gate))
-
-    conv(hpad, 1, forward)
-
-    def dw_rows(d):
+    partner = 2 * zi + 1 - yi
+    dz_c, pt_c = [], []
+
+    z_order = [2, 1, 3, 0]
+
+    def dw_tile(d, c):
         at = pl.ds(pl.multiple_of(d * block, 64), block)
-        return jnp.dot(cot_t[at], act[...], preferred_element_type=f32)
-
-    z_order = [2, 1, 3, 0] if n_z == 4 else list(range(1, n_z)) + [0]
-    partner = 2 * zi + 1 - yi
-    dy_c, dz_c, pt_c = [], [], []
-
-    def dy_step(kz):
-        zt = lax.rem(zi + kz, n_z)
-        dy_send[kz] = dw_rows(2 * zt + 1 - yi).astype(bf16)
-        c = send(dy_send.at[kz], dy_got.at[kz], dy_s.at[kz], dy_r.at[kz], dp=partner)
-        c.start()
-        dy_c.append(c)
+        return jnp.dot(cot_t[at], act[:, columns(c)], preferred_element_type=f32)
+
+    def dy_tile(kz, c):
+        return send(dy_send.at[kz, c], dy_got.at[kz, c], dy_s.at[kz, c], dy_r.at[kz, c], dp=partner)
+
+    def dy_step(kz, c):
+        dy_send[kz, c] = dw_tile(2 * lax.rem(zi + kz, n_z) + 1 - yi, c).astype(bf16)
+        dy_tile(kz, c).start()
 
     def dz_step(kz):
         zt = lax.rem(zi + kz, n_z)
-        arrived(dy_got.at[kz], dy_s.at[kz], dy_r.at[kz], dp=partner)
-        total = dw_rows(2 * zt + yi) + dy_got[kz].astype(f32)
+        for c in range(tiles):
+            dy_tile(kz, c).wait_recv()
+            total = dw_tile(2 * zt + yi, c) + dy_got[kz, c].astype(f32)
+            if kz:
+                dz_send[kz, c] = total.astype(bf16)
+            else:
+                dz_own[c] = total
         if kz:
-            dz_send[kz] = total.astype(bf16)
             c = send(dz_send.at[kz], dz_got.at[kz], dz_s.at[kz], dz_r.at[kz], dp=2 * zt + yi)
             c.start()
             dz_c.append(c)
-        else:
-            dz_own[...] = total
-
-    for kz in z_order[:-2]:
-        dy_step(kz)
+
+    def forward(c, carry):
+        cs = columns(c)
+        weights = taps[:, cs]
+        for base in range(0, ROWS, chunk):
+            rows = slice(base, base + chunk)
+            total = jnp.zeros((chunk, 128), f32)
+            for j in range(KERNEL):
+                start = pad + base + j - centre
+                total = total + weights[j : j + 1] * (hpad[c, start : start + chunk] * masks[j, rows])
+            gate = 1.0 / (1.0 + jnp.exp(-total))
+            act[rows, cs] = (total * gate).astype(bf16)
+            gpad[c, pad + base : pad + base + chunk] = gact[rows, cs] * gate * (1.0 + total * (1.0 - gate))
+        for kz in z_order[:-2]:
+            dy_step(kz, c)
+        return carry
+
+    lax.fori_loop(0, tiles, forward, 0)
     for k in [2, 3, 1, 0]:
         at = pl.ds(pl.multiple_of(mp_peer(k) * width, 128), width)
         part[k] = lax.dot_general(
@@ -398,11 +396,11 @@
         weights = taps[:, cs]
         for base in range(0, ROWS, chunk):
             rows = slice(base, base + chunk)
-            values = hpad[pad + base : pad + base + chunk, cs]
+            values = hpad[c, pad + base : pad + base + chunk]
             total = cot_all[mine, rows, cs].astype(f32)
             for j in range(KERNEL):
                 start = pad + base - (j - centre)
-                taken = gpad[start : start + chunk, cs] * masks[KERNEL - 1 - j, rows]
+                taken = gpad[c, start : start + chunk] * masks[KERNEL - 1 - j, rows]
                 total = total + weights[j : j + 1] * taken
                 sums = jnp.sum((values * taken).reshape(chunk // 8, 8, 128), axis=0)
                 tap_acc[j] = sums if base == 0 else tap_acc[j] + sums
@@ -411,7 +409,6 @@
             gfull[features + j : features + j + 1, cs] = jnp.sum(tap_acc[j], axis=0, keepdims=True)
         return carry
 
-    tiles = width // 128
     lax.fori_loop(0, tiles - 1, backward, 0)
     dz_step(z_order[0])
     lax.fori_loop(tiles - 1, tiles, backward, 0)
@@ -431,7 +428,8 @@
 
     push(gs.at[1 - yi], gy_got, gy_s.at[0], gy_r.at[0], partner)
     for kz in z_order[-2:]:
-        dy_step(kz)
+        for c in range(tiles):
+            dy_step(kz, c)
     for kz in z_order[1:-2]:
         dz_step(kz)
     arrived(gy_got, gy_s.at[0], gy_r.at[0], dp=partner)
@@ -457,7 +455,9 @@
     for k in range(1, n_mp):
         arrived(part_got.at[k], pt_s.at[k], pt_r.at[k], mp=mp_from(k))
         branch = branch + part_got[k].astype(f32)
-    out_ref[...] = (hpad[pad : pad + ROWS] + branch).astype(out_ref.dtype)
+    for c in range(tiles):
+        part_c = branch[:, c * 128 : (c + 1) * 128]
+        out_ref[:, c * 128 : (c + 1) * 128] = (hpad[c, pad : pad + ROWS] + part_c).astype(out_ref.dtype)
     for kz in range(1, n_z):
         src = lax.rem(zi + n_z - kz, n_z)
         arrived(gall.at[yi, src], ga_s.at[kz], ga_r.at[kz], dp=2 * src + yi)
@@ -467,7 +467,8 @@
         src = 2 * lax.rem(zi + n_z - kz, n_z) + yi
         arrived(dz_got.at[kz], dz_s.at[kz], dz_r.at[kz], dp=src)
         total = total + dz_got[kz].astype(f32)
-    gout_ref[...] = scale * total
+    for c in range(tiles):
+        gout_ref[:, c * 128 : (c + 1) * 128] = scale * total[c]
     for kz in range(n_z):
         src = lax.rem(zi + n_z - kz, n_z)
         arrived(gall.at[1 - yi, src], gb_s.at[kz], gb_r.at[kz], dp=partner)
@@ -481,7 +482,10 @@
                 gin_ref[at : at + low] = values[:low]
             if high > low:
                 gdep_ref[at + low - features : at + high - features] = values[low:high]
-    for c in tab_c + fr_c + ct_c + cp_c + dy_c + pt_c + dz_c + g_c:
+    for kz in range(n_z):
+        for c in range(tiles):
+            dy_tile(kz, c).wait_send()
+    for c in tab_c + fr_c + ct_c + cp_c + pt_c + dz_c + g_c:
         c.wait_send()
 
 
@@ -508,6 +512,7 @@
     f32, bf16 = jnp.float32, jnp.bfloat16
     vm = pltpu.VMEM
     i32 = jnp.int32
+    tiles = width // 128
     scratch = [
         vm((features, src_rows), bf16),
         vm((1, entries), i32),
@@ -527,18 +532,18 @@
         vm((ROWS + 32, 128), f32),
         vm((KERNEL, ROWS, 128), f32),
         vm((32, width), f32),
-        vm((ROWS + 32, width), f32),
+        vm((tiles, ROWS + 32, 128), f32),
         vm((ROWS, width), bf16),
         vm((ROWS, width), f32),
-        vm((ROWS + 32, width), f32),
+        vm((tiles, ROWS + 32, 128), f32),
         vm((ROWS, width), bf16),
         vm((n_mp, ROWS, width), bf16),
         vm((n_mp, ROWS, width), bf16),
-        vm((n_z, block, width), bf16),
-        vm((n_z, block, width), bf16),
-        vm((n_z, block, width), bf16),
-        vm((n_z, block, width), bf16),
-        vm((block, width), f32),
+        vm((n_z, tiles, block, 128), bf16),
+        vm((n_z, tiles, block, 128), bf16),
+        vm((n_z, tiles, block, 128), bf16),
+        vm((n_z, tiles, block, 128), bf16),
+        vm((tiles, block, 128), f32),
         vm((n_dp * strip, width), f32),
         vm((KERNEL, 8, 128), f32),
         vm((2, n_z, strip, width), bf16),
@@ -547,10 +552,10 @@
         vm((n_z, strip, width), bf16),
         vm((2, n_z, strip, width), bf16),
     ]
-    for count in (n_dp, n_dp, n_mp, n_mp, n_mp, n_z, n_z, 1, n_z, n_z, n_z):
-        scratch += [pltpu.SemaphoreType.DMA((count,)), pltpu.SemaphoreType.DMA((count,))]
+    for shape in ((n_dp,), (n_dp,), (n_mp,), (n_mp,), (n_mp,), (n_z, tiles), (n_z,), (1,), (n_z,), (n_z,), (n_z,)):
+        scratch += [pltpu.SemaphoreType.DMA(shape), pltpu.SemaphoreType.DMA(shape)]
     whole = pl.BlockSpec(memory_space=pltpu.VMEM)
-    remote = pl.BlockSpec(memory_space=pltpu.HBM)
+    remote = pl.BlockSpec(memory_space=pl.ANY)
     results = pl.pallas_call(
         functools.partial(fused_kernel, n_dp, n_mp, 1.0 / math.sqrt(n_dp * ROWS)),
         out_shape=(
@@ -563,15 +568,16 @@
         out_specs=(whole,) * 4,
         scratch_shapes=scratch,
         compiler_params=pltpu.CompilerParams(
-            collective_id=0, has_side_effects=True, vmem_limit_bytes=48 * 1024 * 1024
+            collective_id=0, has_side_effects=True, vmem_limit_bytes=62 * 1024 * 1024
         ),
     )(frames.T, lengths, destinations, offsets, in_weight, depth_weight, out_weight, cotangent)
     return pl.pallas_call(
         store_kernel,
         out_shape=tuple(jax.ShapeDtypeStruct(r.shape, r.dtype) for r in results),
-        in_specs=[whole] * 4,
+        in_specs=[remote] * 4,
         out_specs=(remote,) * 4,
         scratch_shapes=[pltpu.SemaphoreType.DMA((4,))],
+        compiler_params=pltpu.CompilerParams(vmem_limit_bytes=62 * 1024 * 1024),
     )(*results)
 
 

time: 67.6 us -> 86.1 us (1.27)
  Pallas kernels: 56.9 us -> 85.3 us
  local copies, waits for them, and re-layouts: 9.7 us -> 0 us
    pallas_call x1, Pallas kernels: 2.21 us -> 32.4 us  [fused(): pl.pallas_call(store_kernel, out_shape=tuple((jax.ShapeDtypeStruct(r.shap...]
    unnamed x24 -> x0, local copies, waits for them, and re-layouts: 9.7 us -> none
    pallas_call x1, Pallas kernels: 54.7 us -> 52.9 us  [fused(): pl.pallas_call(functools.partial(fused_kernel, n_dp, n_mp, 1.0 / math.sqr...]
where the time goes in v3:
time: 86.1 us; the launch traced here: 86 us
  Pallas kernels  85.3 us (99%)
    pallas_call x1, Pallas kernels, fused(): pl.pallas_call(functools.partial(fused_kernel, n_dp, n_mp, 1.0 / math.sqr...  52.9 us
    pallas_call x1, Pallas kernels, fused(): pl.pallas_call(store_kernel, out_shape=tuple((jax.ShapeDtypeStruct(r.shap...  32.4 us

profile of v3, /device:TPU:0, one launch (start us, length us, event | category | flops | bytes accessed | tf_op | source)
XLA Modules:
  0.0 86.0 jit_solution(2903424591153904861)
XLA Ops:
  0.6 52.9 %shard_map.111 = (bf16[256,384]{1,0:T(8,128)(2,1)}, f32[320,384]{1,0:T(8,128)}, f32[31,384]{1,0:T(8,128)}, f32[192,384]{1,0:T(8,128)}) custom-call(bf16[320,1024]{1,0:T(8,128)(2,1)} %bitcast.1, s32[1,128]{1,0:T(1,128)} %lens_in.1, s32[1,128]{1,0:T(1,128)} %dests_in.1, s32[1,128]{1,0:T(1,128)} %offs_in.1, bf16[320,384]{1,0:T(8,128)(2,1)} %w_in_in.1, ...), custom_call_target="tpu_custom_call" | custom-call | tf_op jit(solution)/shard_map/pallas_call | solution.py:559
  53.6 32.4 %shard_map.112 = (bf16[256,384]{1,0:T(8,128)(2,1)}, f32[320,384]{1,0:T(8,128)}, f32[31,384]{1,0:T(8,128)}, f32[192,384]{1,0:T(8,128)}) custom-call(bf16[256,384]{1,0:T(8,128)(2,1)} %get-tuple-element.8.refs_0_, f32[320,384]{1,0:T(8,128)} %get-tuple-element.9.refs_1_, f32[31,384]{1,0:T(8,128)} %get-tuple-element.10.refs_2_, f32[192,384]{1,0:T(8,128)} %get-tuple-element.11.refs_3_), custom_call_target="tpu_custom_call" | custom-call | tf_op jit(solution)/shard_map/pallas_call | solution.py:574

commit v4 on v3

--- a/solution.py
+++ b/solution.py
@@ -574,7 +574,7 @@
     return pl.pallas_call(
         store_kernel,
         out_shape=tuple(jax.ShapeDtypeStruct(r.shape, r.dtype) for r in results),
-        in_specs=[remote] * 4,
+        in_specs=[whole] * 4,
         out_specs=(remote,) * 4,
         scratch_shapes=[pltpu.SemaphoreType.DMA((4,))],
         compiler_params=pltpu.CompilerParams(vmem_limit_bytes=62 * 1024 * 1024),

time: 86.1 us -> 56 us (0.65)
  Pallas kernels: 85.3 us -> 55.1 us
    pallas_call x1, Pallas kernels: 32.4 us -> 2.21 us  [fused(): pl.pallas_call(store_kernel, out_shape=tuple((jax.ShapeDtypeStruct(r.shap...]
where the time goes in v4:
time: 56 us; the launch traced here: 55.8 us
  Pallas kernels  55.1 us (98%)
  between operations  0.64 us (1%)
    pallas_call x1, Pallas kernels, fused(): pl.pallas_call(functools.partial(fused_kernel, n_dp, n_mp, 1.0 / math.sqr...  52.9 us
    pallas_call x1, Pallas kernels, fused(): pl.pallas_call(store_kernel, out_shape=tuple((jax.ShapeDtypeStruct(r.shap...  2.21 us

profile of v4, /device:TPU:0, one launch (start us, length us, event | category | flops | bytes accessed | tf_op | source)
XLA Modules:
  0.0 55.8 jit_solution(13271816993172945122)
XLA Ops:
  0.6 52.9 %shard_map.111 = (bf16[256,384]{1,0:T(8,128)(2,1)}, f32[320,384]{1,0:T(8,128)}, f32[31,384]{1,0:T(8,128)}, f32[192,384]{1,0:T(8,128)}) custom-call(bf16[320,1024]{1,0:T(8,128)(2,1)} %bitcast.1, s32[1,128]{1,0:T(1,128)} %lens_in.1, s32[1,128]{1,0:T(1,128)} %dests_in.1, s32[1,128]{1,0:T(1,128)} %offs_in.1, bf16[320,384]{1,0:T(8,128)(2,1)} %w_in_in.1, ...), custom_call_target="tpu_custom_call" | custom-call | tf_op jit(solution)/shard_map/pallas_call | solution.py:559
  53.6 2.2 %shard_map.112 = (bf16[256,384]{1,0:T(8,128)(2,1)}, f32[320,384]{1,0:T(8,128)}, f32[31,384]{1,0:T(8,128)}, f32[192,384]{1,0:T(8,128)}) custom-call(bf16[256,384]{1,0:T(8,128)(2,1)} %get-tuple-element.8.refs_0_, f32[320,384]{1,0:T(8,128)} %get-tuple-element.9.refs_1_, f32[31,384]{1,0:T(8,128)} %get-tuple-element.10.refs_2_, f32[192,384]{1,0:T(8,128)} %get-tuple-element.11.refs_3_), custom_call_target="tpu_custom_call" | custom-call | tf_op jit(solution)/shard_map/pallas_call | solution.py:574

commit v5 on v4

--- a/solution.py
+++ b/solution.py
@@ -140,9 +140,9 @@
     frames_in, lens_in, dests_in, offs_in, w_in_in, w_depth_in, w_out_in, cot_in,
     out_ref, gin_ref, gdep_ref, gout_ref,
     frames, lens, dests, offs, w_in, w_depth, w_out, in_sem,
-    tables, slots, got, comp_all, cot_all, cot_t, packed, lab_pad, masks, taps, hpad, act, gact, gpad, ghid,
-    part, part_got, dy_send, dy_got, dz_send, dz_got, dz_own, gfull, tap_acc, gs, gy_got, gz_send, gz_got, gall,
-    tab_s, tab_r, fr_s, fr_r, cp_s, cp_r, ct_s, ct_r, pt_s, pt_r, dy_s, dy_r, dz_s, dz_r, gy_s, gy_r, gz_s, gz_r, ga_s, ga_r, gb_s, gb_r,
+    tables, slots, got, comp_all, cot_all, cot_t, packed, lab_pad, masks, taps, hpad, act, pact, own_t, pcot, gact, gpad, ghid,
+    part, part_got, dz_send, dz_got, dz_own, gfull, tap_acc, gs, gy_got, gz_send, gz_got, gall,
+    tab_s, tab_r, fr_s, fr_r, cp_s, cp_r, ct_s, ct_r, pc_s, pc_r, pt_s, pt_r, ac_s, ac_r, dz_s, dz_r, gy_s, gy_r, gz_s, gz_r, ga_s, ga_r, gb_s, gb_r,
 ):
     f32, bf16 = jnp.float32, jnp.bfloat16
     me = lax.axis_index("dp")
@@ -240,6 +240,11 @@
         ct_c.append(c)
     for load in loads[4:]:
         load.wait()
+    partner = 2 * zi + 1 - yi
+    own_t[...] = cot_all[mine].T.reshape(2, block, ROWS)
+    c = send(own_t.at[1 - yi], pcot.at[mine], pc_s.at[0], pc_r.at[0], dp=partner)
+    c.start()
+    ct_c.append(c)
 
     taps[0:KERNEL] = w_depth[...].astype(f32)
     for ref in (hpad, gpad):
@@ -302,6 +307,12 @@
         c.start()
         cp_c.append(c)
 
+    arrived(pcot.at[mine], pc_s.at[0], pc_r.at[0], dp=partner)
+    for k in range(1, n_mp):
+        c = send(pcot.at[mine], pcot.at[mine], pc_s.at[k], pc_r.at[k], mp=mp_peer(k))
+        c.start()
+        ct_c.append(c)
+
     arrived(cot_all.at[across], ct_s.at[0], ct_r.at[0], mp=across)
     c = send(cot_all.at[across], cot_all.at[across], ct_s.at[2], ct_r.at[2], mp=sibling)
     c.start()
@@ -334,27 +345,19 @@
     def columns(c):
         return pl.ds(pl.multiple_of(c * 128, 128), 128)
 
-    partner = 2 * zi + 1 - yi
     dz_c, pt_c = [], []
 
     z_order = [2, 1, 3, 0]
 
-    def dw_tile(d, c):
-        at = pl.ds(pl.multiple_of(d * block, 64), block)
-        return jnp.dot(cot_t[at], act[:, columns(c)], preferred_element_type=f32)
-
-    def dy_tile(kz, c):
-        return send(dy_send.at[kz, c], dy_got.at[kz, c], dy_s.at[kz, c], dy_r.at[kz, c], dp=partner)
-
-    def dy_step(kz, c):
-        dy_send[kz, c] = dw_tile(2 * lax.rem(zi + kz, n_z) + 1 - yi, c).astype(bf16)
-        dy_tile(kz, c).start()
+    def act_tile(c):
+        return send(act.at[c], pact.at[c], ac_s.at[c], ac_r.at[c], dp=partner)
 
     def dz_step(kz):
         zt = lax.rem(zi + kz, n_z)
+        at = pl.ds(pl.multiple_of((2 * zt + yi) * block, 64), block)
         for c in range(tiles):
-            dy_tile(kz, c).wait_recv()
-            total = dw_tile(2 * zt + yi, c) + dy_got[kz, c].astype(f32)
+            total = jnp.dot(cot_t[at], act[c], preferred_element_type=f32)
+            total = total + jnp.dot(pcot[zt], pact[c], preferred_element_type=f32)
             if kz:
                 dz_send[kz, c] = total.astype(bf16)
             else:
@@ -374,22 +377,30 @@
                 start = pad + base + j - centre
                 total = total + weights[j : j + 1] * (hpad[c, start : start + chunk] * masks[j, rows])
             gate = 1.0 / (1.0 + jnp.exp(-total))
-            act[rows, cs] = (total * gate).astype(bf16)
+            act[c, rows] = (total * gate).astype(bf16)
             gpad[c, pad + base : pad + base + chunk] = gact[rows, cs] * gate * (1.0 + total * (1.0 - gate))
-        for kz in z_order[:-2]:
-            dy_step(kz, c)
+        act_tile(c).start()
         return carry
 
     lax.fori_loop(0, tiles, forward, 0)
+    activated = jnp.concatenate([act[c] for c in range(tiles)], 1)
     for k in [2, 3, 1, 0]:
         at = pl.ds(pl.multiple_of(mp_peer(k) * width, 128), width)
         part[k] = lax.dot_general(
-            act[...], w_out[at], (((1,), (1,)), ((), ())), preferred_element_type=f32
+            activated, w_out[at], (((1,), (1,)), ((), ())), preferred_element_type=f32
         ).astype(bf16)
         if k:
             c = send(part.at[k], part_got.at[k], pt_s.at[k], pt_r.at[k], mp=mp_peer(k))
             c.start()
             pt_c.append(c)
+
+    for k in range(1, n_mp):
+        src = mp_from(k)
+        arrived(pcot.at[src], pc_s.at[k], pc_r.at[k], mp=src)
+    for c in range(tiles):
+        act_tile(c).wait_recv()
+    for kz in z_order[:-2]:
+        dz_step(kz)
 
     def backward(c, carry):
         cs = columns(c)
@@ -409,9 +420,7 @@
             gfull[features + j : features + j + 1, cs] = jnp.sum(tap_acc[j], axis=0, keepdims=True)
         return carry
 
-    lax.fori_loop(0, tiles - 1, backward, 0)
-    dz_step(z_order[0])
-    lax.fori_loop(tiles - 1, tiles, backward, 0)
+    lax.fori_loop(0, tiles, backward, 0)
     gfull[0:features] = lax.dot_general(
         packed[...], ghid[...], (((0,), (0,)), ((), ())), preferred_element_type=f32
     )
@@ -427,11 +436,6 @@
         g_c.append(c)
 
     push(gs.at[1 - yi], gy_got, gy_s.at[0], gy_r.at[0], partner)
-    for kz in z_order[-2:]:
-        for c in range(tiles):
-            dy_step(kz, c)
-    for kz in z_order[1:-2]:
-        dz_step(kz)
     arrived(gy_got, gy_s.at[0], gy_r.at[0], dp=partner)
     for kz in z_order:
         zt = lax.rem(zi + kz, n_z)
@@ -482,9 +486,8 @@
                 gin_ref[at : at + low] = values[:low]
             if high > low:
                 gdep_ref[at + low - features : at + high - features] = values[low:high]
-    for kz in range(n_z):
-        for c in range(tiles):
-            dy_tile(kz, c).wait_send()
+    for c in range(tiles):
+        act_tile(c).wait_send()
     for c in tab_c + fr_c + ct_c + cp_c + pt_c + dz_c + g_c:
         c.wait_send()
 
@@ -533,14 +536,15 @@
         vm((KERNEL, ROWS, 128), f32),
         vm((32, width), f32),
         vm((tiles, ROWS + 32, 128), f32),
-        vm((ROWS, width), bf16),
+        vm((tiles, ROWS, 128), bf16),
+        vm((tiles, ROWS, 128), bf16),
+        vm((2, block, ROWS), bf16),
+        vm((n_mp, block, ROWS), bf16),
         vm((ROWS, width), f32),
         vm((tiles, ROWS + 32, 128), f32),
         vm((ROWS, width), bf16),
         vm((n_mp, ROWS, width), bf16),
         vm((n_mp, ROWS, width), bf16),
-        vm((n_z, tiles, block, 128), bf16),
-        vm((n_z, tiles, block, 128), bf16),
         vm((n_z, tiles, block, 128), bf16),
         vm((n_z, tiles, block, 128), bf16),
         vm((tiles, block, 128), f32),
@@ -552,7 +556,7 @@
         vm((n_z, strip, width), bf16),
         vm((2, n_z, strip, width), bf16),
     ]
-    for shape in ((n_dp,), (n_dp,), (n_mp,), (n_mp,), (n_mp,), (n_z, tiles), (n_z,), (1,), (n_z,), (n_z,), (n_z,)):
+    for shape in ((n_dp,), (n_dp,), (n_mp,), (n_mp,), (n_mp,), (n_mp,), (tiles,), (n_z,), (1,), (n_z,), (n_z,), (n_z,)):
         scratch += [pltpu.SemaphoreType.DMA(shape), pltpu.SemaphoreType.DMA(shape)]
     whole = pl.BlockSpec(memory_space=pltpu.VMEM)
     remote = pl.BlockSpec(memory_space=pl.ANY)
@@ -582,7 +586,7 @@
 
 
 def solution(mesh):
-    small = mesh.shape["dp"] == 8 and mesh.shape["mp"] == 4
+    small = mesh.shape["dp"] == 2 * mesh.shape["mp"] == 8
     placed = (
         P("dp", None),
         P("dp", None),

time: 56 us -> 55.5 us (level)
  no operation moved by 1% of the time
where the time goes in v5:
time: 55.5 us; the launch traced here: 55.3 us
  Pallas kernels  54.7 us (99%)
  between operations  0.64 us (1%)
    pallas_call x1, Pallas kernels, fused(): pl.pallas_call(functools.partial(fused_kernel, n_dp, n_mp, 1.0 / math.sqr...  52.5 us
    pallas_call x1, Pallas kernels, fused(): pl.pallas_call(store_kernel, out_shape=tuple((jax.ShapeDtypeStruct(r.shap...  2.21 us

profile of v5, /device:TPU:0, one launch (start us, length us, event | category | flops | bytes accessed | tf_op | source)
XLA Modules:
  0.0 55.3 jit_solution(8085377587940087537)
XLA Ops:
  0.6 52.5 %shard_map.111 = (bf16[256,384]{1,0:T(8,128)(2,1)}, f32[320,384]{1,0:T(8,128)}, f32[31,384]{1,0:T(8,128)}, f32[192,384]{1,0:T(8,128)}) custom-call(bf16[320,1024]{1,0:T(8,128)(2,1)} %bitcast.1, s32[1,128]{1,0:T(1,128)} %lens_in.1, s32[1,128]{1,0:T(1,128)} %dests_in.1, s32[1,128]{1,0:T(1,128)} %offs_in.1, bf16[320,384]{1,0:T(8,128)(2,1)} %w_in_in.1, ...), custom_call_target="tpu_custom_call" | custom-call | tf_op jit(solution)/shard_map/pallas_call | solution.py:563
  53.1 2.2 %shard_map.112 = (bf16[256,384]{1,0:T(8,128)(2,1)}, f32[320,384]{1,0:T(8,128)}, f32[31,384]{1,0:T(8,128)}, f32[192,384]{1,0:T(8,128)}) custom-call(bf16[256,384]{1,0:T(8,128)(2,1)} %get-tuple-element.8.refs_0_, f32[320,384]{1,0:T(8,128)} %get-tuple-element.9.refs_1_, f32[31,384]{1,0:T(8,128)} %get-tuple-element.10.refs_2_, f32[192,384]{1,0:T(8,128)} %get-tuple-element.11.refs_3_), custom_call_target="tpu_custom_call" | custom-call | tf_op jit(solution)/shard_map/pallas_call | solution.py:578

commit v6 on v5

--- a/solution.py
+++ b/solution.py
@@ -140,8 +140,8 @@
     frames_in, lens_in, dests_in, offs_in, w_in_in, w_depth_in, w_out_in, cot_in,
     out_ref, gin_ref, gdep_ref, gout_ref,
     frames, lens, dests, offs, w_in, w_depth, w_out, in_sem,
-    tables, slots, got, comp_all, cot_all, cot_t, packed, lab_pad, masks, taps, hpad, act, pact, own_t, pcot, gact, gpad, ghid,
-    part, part_got, dz_send, dz_got, dz_own, gfull, tap_acc, gs, gy_got, gz_send, gz_got, gall,
+    tables, slots, got, comp_all, cot_all, cot_t, packed_t, lab_pad, masks, taps, hpad, act, pact, own_t, pcot, gact, gpad, ghid,
+    part, part_got, dz_send, dz_got, dz_own, gfull, g_own, tap_acc, gs, gy_got, gz_send, gz_got, gall,
     tab_s, tab_r, fr_s, fr_r, cp_s, cp_r, ct_s, ct_r, pc_s, pc_r, pt_s, pt_r, ac_s, ac_r, dz_s, dz_r, gy_s, gy_r, gz_s, gz_r, ga_s, ga_r, gb_s, gb_r,
 ):
     f32, bf16 = jnp.float32, jnp.bfloat16
@@ -154,7 +154,7 @@
     width = cot_all.shape[2]
     entries = lens.shape[1]
     block = gout_ref.shape[0]
-    strip = gs.shape[2]
+    strip = gs.shape[3]
     centre = (KERNEL - 1) // 2
     pad = 16
     n_z = n_dp // 2
@@ -337,8 +337,9 @@
         src = mp_from(k)
         arrived(comp_all.at[src], cp_s.at[k], cp_r.at[k], mp=src)
     everything = jnp.concatenate([comp_all[b] for b in range(n_mp)], 0)
-    packed[...] = jnp.dot(pick_rows, everything, preferred_element_type=f32).astype(bf16)
-    hidden = jnp.dot(packed[...], w_in[...], preferred_element_type=f32).astype(bf16).astype(f32)
+    packed = jnp.dot(pick_rows, everything, preferred_element_type=f32).astype(bf16)
+    packed_t[...] = packed.T
+    hidden = jnp.dot(packed, w_in[...], preferred_element_type=f32).astype(bf16).astype(f32)
     for c in range(tiles):
         hpad[c, pad : pad + ROWS] = hidden[:, c * 128 : (c + 1) * 128]
 
@@ -402,8 +403,15 @@
     for kz in z_order[:-2]:
         dz_step(kz)
 
-    def backward(c, carry):
-        cs = columns(c)
+    g_c = []
+
+    def push(src, dst, ssem, rsem, peer):
+        c = send(src, dst, ssem, rsem, dp=peer)
+        c.start()
+        g_c.append(c)
+
+    def backward(c):
+        cs = slice(c * 128, (c + 1) * 128)
         weights = taps[:, cs]
         for base in range(0, ROWS, chunk):
             rows = slice(base, base + chunk)
@@ -417,42 +425,55 @@
                 tap_acc[j] = sums if base == 0 else tap_acc[j] + sums
             ghid[rows, cs] = total.astype(bf16)
         for j in range(KERNEL):
-            gfull[features + j : features + j + 1, cs] = jnp.sum(tap_acc[j], axis=0, keepdims=True)
-        return carry
-
-    lax.fori_loop(0, tiles, backward, 0)
-    gfull[0:features] = lax.dot_general(
-        packed[...], ghid[...], (((0,), (0,)), ((), ())), preferred_element_type=f32
-    )
-    for y in range(2):
-        for z in range(n_z):
-            at = (y * n_z + z) * strip
-            gs[y, z] = gfull[at : at + strip].astype(bf16)
-    g_c = []
-
-    def push(src, dst, ssem, rsem, peer):
-        c = send(src, dst, ssem, rsem, dp=peer)
-        c.start()
-        g_c.append(c)
-
-    push(gs.at[1 - yi], gy_got, gy_s.at[0], gy_r.at[0], partner)
-    arrived(gy_got, gy_s.at[0], gy_r.at[0], dp=partner)
-    for kz in z_order:
-        zt = lax.rem(zi + kz, n_z)
-        at = pl.ds(pl.multiple_of((yi * n_z + zt) * strip, 16), strip)
-        total = gfull[at] + gy_got[zt].astype(f32)
-        if kz:
-            gz_send[kz] = total.astype(bf16)
-            push(gz_send.at[kz], gz_got.at[kz], gz_s.at[kz], gz_r.at[kz], 2 * zt + yi)
+            gfull[c, features + j : features + j + 1] = jnp.sum(tap_acc[j], axis=0, keepdims=True)
+        gfull[c, 0:features] = jnp.dot(packed_t[...], ghid[:, cs], preferred_element_type=f32)
+        for y in range(2):
+            for z in range(n_z):
+                at = (y * n_z + z) * strip
+                gs[c, y, z] = gfull[c, at : at + strip].astype(bf16)
+        push(gs.at[c, 1 - yi], gy_got.at[c], gy_s.at[c], gy_r.at[c], partner)
+
+    def over_z(c):
+        arrived(gy_got.at[c], gy_s.at[c], gy_r.at[c], dp=partner)
+        for kz in z_order:
+            zt = lax.rem(zi + kz, n_z)
+            at = pl.ds(pl.multiple_of((yi * n_z + zt) * strip, 16), strip)
+            total = gfull[c, at] + gy_got[c, zt].astype(f32)
+            if kz:
+                gz_send[c, kz] = total.astype(bf16)
+                push(gz_send.at[c, kz], gz_got.at[c, kz], gz_s.at[c, kz], gz_r.at[c, kz], 2 * zt + yi)
+            else:
+                g_own[c] = total
+
+    def back_z(c):
+        total = g_own[c]
+        for kz in range(1, n_z):
+            src = 2 * lax.rem(zi + n_z - kz, n_z) + yi
+            arrived(gz_got.at[c, kz], gz_s.at[c, kz], gz_r.at[c, kz], dp=src)
+            total = total + gz_got[c, kz].astype(f32)
+        gall[c, yi, zi] = total.astype(bf16)
+        mine_at = gall.at[c, yi, zi]
+        for kz in z_order[:-1]:
+            push(mine_at, mine_at, ga_s.at[c, kz], ga_r.at[c, kz], 2 * lax.rem(zi + kz, n_z) + yi)
+        push(mine_at, mine_at, gb_s.at[c, 0], gb_r.at[c, 0], partner)
+
+    def back_y(c):
+        for kz in range(1, n_z):
+            src = lax.rem(zi + n_z - kz, n_z)
+            arrived(gall.at[c, yi, src], ga_s.at[c, kz], ga_r.at[c, kz], dp=2 * src + yi)
+            push(gall.at[c, yi, src], gall.at[c, yi, src], gb_s.at[c, kz], gb_r.at[c, kz], partner)
+
+    for c in range(tiles):
+        backward(c)
+        if c:
+            over_z(c - 1)
     dz_step(z_order[-2])
-    for kz in range(1, n_z):
-        arrived(gz_got.at[kz], gz_s.at[kz], gz_r.at[kz], dp=2 * lax.rem(zi + n_z - kz, n_z) + yi)
-        total = total + gz_got[kz].astype(f32)
-    gall[yi, zi] = total.astype(bf16)
-    for kz in z_order[:-1]:
-        zt = lax.rem(zi + kz, n_z)
-        push(gall.at[yi, zi], gall.at[yi, zi], ga_s.at[kz], ga_r.at[kz], 2 * zt + yi)
-    push(gall.at[yi, zi], gall.at[yi, zi], gb_s.at[0], gb_r.at[0], partner)
+    for c in range(tiles):
+        back_z(c)
+        if c == tiles - 2:
+            over_z(tiles - 1)
+        if c:
+            back_y(c - 1)
     dz_step(0)
 
     branch = part[0].astype(f32)
@@ -462,10 +483,7 @@
     for c in range(tiles):
         part_c = branch[:, c * 128 : (c + 1) * 128]
         out_ref[:, c * 128 : (c + 1) * 128] = (hpad[c, pad : pad + ROWS] + part_c).astype(out_ref.dtype)
-    for kz in range(1, n_z):
-        src = lax.rem(zi + n_z - kz, n_z)
-        arrived(gall.at[yi, src], ga_s.at[kz], ga_r.at[kz], dp=2 * src + yi)
-        push(gall.at[yi, src], gall.at[yi, src], gb_s.at[kz], gb_r.at[kz], partner)
+    back_y(tiles - 1)
     total = dz_own[...]
     for kz in range(1, n_z):
         src = 2 * lax.rem(zi + n_z - kz, n_z) + yi
@@ -473,19 +491,21 @@
         total = total + dz_got[kz].astype(f32)
     for c in range(tiles):
         gout_ref[:, c * 128 : (c + 1) * 128] = scale * total[c]
-    for kz in range(n_z):
-        src = lax.rem(zi + n_z - kz, n_z)
-        arrived(gall.at[1 - yi, src], gb_s.at[kz], gb_r.at[kz], dp=partner)
-    for y in range(2):
-        for z in range(n_z):
-            at = (y * n_z + z) * strip
-            values = scale * gall[y, z].astype(f32)
-            low = min(max(features - at, 0), strip)
-            high = min(max(features + KERNEL - at, 0), strip)
-            if low > 0:
-                gin_ref[at : at + low] = values[:low]
-            if high > low:
-                gdep_ref[at + low - features : at + high - features] = values[low:high]
+    for c in range(tiles):
+        cs = slice(c * 128, (c + 1) * 128)
+        for kz in range(n_z):
+            src = lax.rem(zi + n_z - kz, n_z)
+            arrived(gall.at[c, 1 - yi, src], gb_s.at[c, kz], gb_r.at[c, kz], dp=partner)
+        for y in range(2):
+            for z in range(n_z):
+                at = (y * n_z + z) * strip
+                values = scale * gall[c, y, z].astype(f32)
+                low = min(max(features - at, 0), strip)
+                high = min(max(features + KERNEL - at, 0), strip)
+                if low > 0:
+                    gin_ref[at : at + low, cs] = values[:low]
+                if high > low:
+                    gdep_ref[at + low - features : at + high - features, cs] = values[low:high]
     for c in range(tiles):
         act_tile(c).wait_send()
     for c in tab_c + fr_c + ct_c + cp_c + pt_c + dz_c + g_c:
@@ -531,7 +551,7 @@
         vm((n_mp, sources * quarter, features), bf16),
         vm((n_mp, ROWS, width), bf16),
         vm((model, ROWS), bf16),
-        vm((ROWS, features), bf16),
+        vm((features, ROWS), bf16),
         vm((ROWS + 32, 128), f32),
         vm((KERNEL, ROWS, 128), f32),
         vm((32, width), f32),
@@ -548,15 +568,16 @@
         vm((n_z, tiles, block, 128), bf16),
         vm((n_z, tiles, block, 128), bf16),
         vm((tiles, block, 128), f32),
-        vm((n_dp * strip, width), f32),
+        vm((tiles, n_dp * strip, 128), f32),
+        vm((tiles, strip, 128), f32),
         vm((KERNEL, 8, 128), f32),
-        vm((2, n_z, strip, width), bf16),
-        vm((n_z, strip, width), bf16),
-        vm((n_z, strip, width), bf16),
-        vm((n_z, strip, width), bf16),
-        vm((2, n_z, strip, width), bf16),
+        vm((tiles, 2, n_z, strip, 128), bf16),
+        vm((tiles, n_z, strip, 128), bf16),
+        vm((tiles, n_z, strip, 128), bf16),
+        vm((tiles, n_z, strip, 128), bf16),
+        vm((tiles, 2, n_z, strip, 128), bf16),
     ]
-    for shape in ((n_dp,), (n_dp,), (n_mp,), (n_mp,), (n_mp,), (n_mp,), (tiles,), (n_z,), (1,), (n_z,), (n_z,), (n_z,)):
+    for shape in ((n_dp,), (n_dp,), (n_mp,), (n_mp,), (n_mp,), (n_mp,), (tiles,), (n_z,), (tiles,)) + ((tiles, n_z),) * 3:
         scratch += [pltpu.SemaphoreType.DMA(shape), pltpu.SemaphoreType.DMA(shape)]
     whole = pl.BlockSpec(memory_space=pltpu.VMEM)
     remote = pl.BlockSpec(memory_space=pl.ANY)

time: 55.5 us -> 58.1 us (1.047)
  Pallas kernels: 54.7 us -> 57.3 us
    pallas_call x1, Pallas kernels: 52.5 us -> 55.1 us  [fused(): pl.pallas_call(functools.partial(fused_kernel, n_dp, n_mp, 1.0 / math.sqr...]
where the time goes in v6:
time: 58.1 us; the launch traced here: 58 us
  Pallas kernels  57.3 us (99%)
  between operations  0.64 us (1%)
    pallas_call x1, Pallas kernels, fused(): pl.pallas_call(functools.partial(fused_kernel, n_dp, n_mp, 1.0 / math.sqr...  55.1 us
    pallas_call x1, Pallas kernels, fused(): pl.pallas_call(store_kernel, out_shape=tuple((jax.ShapeDtypeStruct(r.shap...  2.21 us

profile of v6, /device:TPU:0, one launch (start us, length us, event | category | flops | bytes accessed | tf_op | source)
XLA Modules:
  0.0 58.0 jit_solution(5978289729335656855)
XLA Ops:
  0.6 55.1 %shard_map.111 = (bf16[256,384]{1,0:T(8,128)(2,1)}, f32[320,384]{1,0:T(8,128)}, f32[31,384]{1,0:T(8,128)}, f32[192,384]{1,0:T(8,128)}) custom-call(bf16[320,1024]{1,0:T(8,128)(2,1)} %bitcast.1, s32[1,128]{1,0:T(1,128)} %lens_in.1, s32[1,128]{1,0:T(1,128)} %dests_in.1, s32[1,128]{1,0:T(1,128)} %offs_in.1, bf16[320,384]{1,0:T(8,128)(2,1)} %w_in_in.1, ...), custom_call_target="tpu_custom_call" | custom-call | tf_op jit(solution)/shard_map/pallas_call | solution.py:584
  55.7 2.2 %shard_map.112 = (bf16[256,384]{1,0:T(8,128)(2,1)}, f32[320,384]{1,0:T(8,128)}, f32[31,384]{1,0:T(8,128)}, f32[192,384]{1,0:T(8,128)}) custom-call(bf16[256,384]{1,0:T(8,128)(2,1)} %get-tuple-element.8.refs_0_, f32[320,384]{1,0:T(8,128)} %get-tuple-element.9.refs_1_, f32[31,384]{1,0:T(8,128)} %get-tuple-element.10.refs_2_, f32[192,384]{1,0:T(8,128)} %get-tuple-element.11.refs_3_), custom_call_target="tpu_custom_call" | custom-call | tf_op jit(solution)/shard_map/pallas_call | solution.py:599

commit v7 on v5

--- a/solution.py
+++ b/solution.py
@@ -383,25 +383,6 @@
         return carry
 
     lax.fori_loop(0, tiles, forward, 0)
-    activated = jnp.concatenate([act[c] for c in range(tiles)], 1)
-    for k in [2, 3, 1, 0]:
-        at = pl.ds(pl.multiple_of(mp_peer(k) * width, 128), width)
-        part[k] = lax.dot_general(
-            activated, w_out[at], (((1,), (1,)), ((), ())), preferred_element_type=f32
-        ).astype(bf16)
-        if k:
-            c = send(part.at[k], part_got.at[k], pt_s.at[k], pt_r.at[k], mp=mp_peer(k))
-            c.start()
-            pt_c.append(c)
-
-    for k in range(1, n_mp):
-        src = mp_from(k)
-        arrived(pcot.at[src], pc_s.at[k], pc_r.at[k], mp=src)
-    for c in range(tiles):
-        act_tile(c).wait_recv()
-    for kz in z_order[:-2]:
-        dz_step(kz)
-
     def backward(c, carry):
         cs = columns(c)
         weights = taps[:, cs]
@@ -420,7 +401,14 @@
             gfull[features + j : features + j + 1, cs] = jnp.sum(tap_acc[j], axis=0, keepdims=True)
         return carry
 
-    lax.fori_loop(0, tiles, backward, 0)
+    lax.fori_loop(0, 1, backward, 0)
+    for k in range(1, n_mp):
+        src = mp_from(k)
+        arrived(pcot.at[src], pc_s.at[k], pc_r.at[k], mp=src)
+    for c in range(tiles):
+        act_tile(c).wait_recv()
+    dz_step(z_order[0])
+    lax.fori_loop(1, tiles, backward, 0)
     gfull[0:features] = lax.dot_general(
         packed[...], ghid[...], (((0,), (0,)), ((), ())), preferred_element_type=f32
     )
@@ -436,6 +424,18 @@
         g_c.append(c)
 
     push(gs.at[1 - yi], gy_got, gy_s.at[0], gy_r.at[0], partner)
+    dz_step(z_order[1])
+    activated = jnp.concatenate([act[c] for c in range(tiles)], 1)
+    for k in [2, 3, 1, 0]:
+        at = pl.ds(pl.multiple_of(mp_peer(k) * width, 128), width)
+        part[k] = lax.dot_general(
+            activated, w_out[at], (((1,), (1,)), ((), ())), preferred_element_type=f32
+        ).astype(bf16)
+        if k:
+            c = send(part.at[k], part_got.at[k], pt_s.at[k], pt_r.at[k], mp=mp_peer(k))
+            c.start()
+            pt_c.append(c)
+
     arrived(gy_got, gy_s.at[0], gy_r.at[0], dp=partner)
     for kz in z_order:
         zt = lax.rem(zi + kz, n_z)

time: 55.5 us -> 56.4 us (1.016)
  Pallas kernels: 54.7 us -> 55.6 us
    pallas_call x1, Pallas kernels: 52.5 us -> 53.4 us  [fused(): pl.pallas_call(functools.partial(fused_kernel, n_dp, n_mp, 1.0 / math.sqr...]
where the time goes in v7:
time: 56.4 us; the launch traced here: 56.2 us
  Pallas kernels  55.6 us (99%)
  between operations  0.64 us (1%)
    pallas_call x1, Pallas kernels, fused(): pl.pallas_call(functools.partial(fused_kernel, n_dp, n_mp, 1.0 / math.sqr...  53.4 us
    pallas_call x1, Pallas kernels, fused(): pl.pallas_call(store_kernel, out_shape=tuple((jax.ShapeDtypeStruct(r.shap...  2.21 us

profile of v7, /device:TPU:0, one launch (start us, length us, event | category | flops | bytes accessed | tf_op | source)
XLA Modules:
  0.0 56.2 jit_solution(6743160246497143619)
XLA Ops:
  0.6 53.4 %shard_map.111 = (bf16[256,384]{1,0:T(8,128)(2,1)}, f32[320,384]{1,0:T(8,128)}, f32[31,384]{1,0:T(8,128)}, f32[192,384]{1,0:T(8,128)}) custom-call(bf16[320,1024]{1,0:T(8,128)(2,1)} %bitcast.1, s32[1,128]{1,0:T(1,128)} %lens_in.1, s32[1,128]{1,0:T(1,128)} %dests_in.1, s32[1,128]{1,0:T(1,128)} %offs_in.1, bf16[320,384]{1,0:T(8,128)(2,1)} %w_in_in.1, ...), custom_call_target="tpu_custom_call" | custom-call | tf_op jit(solution)/shard_map/pallas_call | solution.py:563
  54.0 2.2 %shard_map.112 = (bf16[256,384]{1,0:T(8,128)(2,1)}, f32[320,384]{1,0:T(8,128)}, f32[31,384]{1,0:T(8,128)}, f32[192,384]{1,0:T(8,128)}) custom-call(bf16[256,384]{1,0:T(8,128)(2,1)} %get-tuple-element.8.refs_0_, f32[320,384]{1,0:T(8,128)} %get-tuple-element.9.refs_1_, f32[31,384]{1,0:T(8,128)} %get-tuple-element.10.refs_2_, f32[192,384]{1,0:T(8,128)} %get-tuple-element.11.refs_3_), custom_call_target="tpu_custom_call" | custom-call | tf_op jit(solution)/shard_map/pallas_call | solution.py:578
